TPU v7x, 32 devices: a whole 2x2x4 slice. The times are simulated.
32 devices in a mesh: groups: 2 (over x), wide: 16 (over z, y, core).
Axes of the slice: x: 2, y: 2, z: 4, core: 2. Of those that a mesh axis runs over, the one named last changes fastest.
Arguments:
- positions: float32 [3, 8192], P(None, 'wide'), may hold values from -4 to 4
- spans: float32 [8192], P('wide'), may hold values from 0.4 to 1
- box_panel: int32 [8192], P('wide'), may hold values from 0 to 63
- panel_dihedral: float32 [64], replicated, may hold values from -3.140625 to 3.140625
- freq_table: float32 [16], replicated, may hold values from 0.2 to 2
- freq_index: int32 [4], P('groups'), parts along dimension 0, may hold values from 0 to 15
- pressures: bfloat16 [4, 2, 8192, 512], P('groups', None, 'wide'), parts along dimension 0, may hold values from -6 to 6
Outputs:
- upwash: float32 [4, 2, 8192, 512], P('groups', None, 'wide'), parts along dimension 0
There are 2 independent parts, one for each index of `groups`. A program takes and returns all parts, laid end to end along the dimension named above; an argument that names none is the same for every part. Nothing has to cross between parts.
All inputs are finite; a program needn't handle non-finite values.
Results may differ from a plain program's by a relative error of at most 0.0029.
Values may be sent and summed in bfloat16 or wider, within the bound.
No kernel may reach another device: no remote copies, remote signals or barrier semaphores. Data moves between devices by JAX's collectives and lax.ppermute only.
A program may use at most 64 MiB of HBM per device.

v0:
```python
import functools

import jax
import jax.numpy as jnp
from jax import lax
from jax.experimental import pallas as pl
from jax.experimental.pallas import tpu as pltpu
from jax.sharding import PartitionSpec as P

SIN_COEF = (6.283182621002197, -41.3414192199707, 81.5961685180664, -76.5799560546875, 41.20474624633789, -12.27022647857666)
COS_COEF = (0.9999992251396179, -19.738981246948242, 64.9287109375, -85.27218627929688, 58.7929573059082, -21.074859619140625)
ROUNDER = 12582912.0
ROWS = 16
LANES = 128


def horner(v, coef):
    value = jnp.full_like(v, coef[-1])
    for c in coef[-2::-1]:
        value = value * v + c
    return value


def shifted(block, axis, distance):
    n = lax.axis_size(axis)
    return lax.ppermute(block, axis, [((i - distance) % n, i) for i in range(n)])


def fill_kernel(recv_ref, send_ref, turns, kern_ref, slot):
    rows, boxes = recv_ref.shape[0], send_ref.shape[1]

    def row_block(i, carry):
        at = pl.ds(pl.multiple_of(i * ROWS, ROWS), ROWS)
        cols = [jnp.broadcast_to(recv_ref[at, q : q + 1], (ROWS, LANES)) for q in range(5)]
        xi, yi, zi, si, ci = cols
        for j in range(boxes // LANES):
            lanes = pl.ds(j * LANES, LANES)
            row = [send_ref[q : q + 1, lanes] for q in range(8)]
            xj, yj, zj, e2, es2, ec2, es, ec = row
            dx, dy, dz = xi - xj, yi - yj, zi - zj
            rho = dy * dy + dz * dz + e2
            d2 = dx * dx + rho
            inv_d = lax.rsqrt(d2)
            inv = pl.reciprocal(rho, approx=True)
            inv = inv * (2.0 - rho * inv)
            dist = d2 * inv_d
            normal_i = ci * dz - si * dy
            normal_j = ec2 * dz - es2 * dy
            planar = ci * ec + si * es
            amp = inv * (planar - normal_i * normal_j * inv) * (1.0 + dx * inv_d)
            lag = dist - dx
            for f, turn in enumerate(turns):
                u = lag * turn
                u = u - ((u + ROUNDER) - ROUNDER)
                v = u * u
                kern_ref[slot, f, 0, at, lanes] = (amp * horner(v, COS_COEF)).astype(jnp.bfloat16)
                kern_ref[slot, f, 1, at, lanes] = (amp * u * horner(v, SIN_COEF)).astype(jnp.bfloat16)
        return carry

    lax.fori_loop(0, rows // ROWS, row_block, 0)


def term_body(freqs, has_acc, turns_ref, recv_ref, send_ref, press_ref, *rest):
    acc_ref = rest[0] if has_acc else None
    out_ref, kern_ref = rest[-2:]
    turns = [turns_ref[f] for f in freqs]
    fill_kernel(recv_ref, send_ref, turns, kern_ref, 0)
    dot = functools.partial(jnp.dot, preferred_element_type=jnp.float32)
    for f in range(len(freqs)):
        kr, ks = kern_ref[0, f, 0], kern_ref[0, f, 1]
        pr, pi = press_ref[f, 0], press_ref[f, 1]
        re = dot(kr, pr) + dot(ks, pi)
        im = dot(kr, pi) - dot(ks, pr)
        if has_acc:
            re = re + acc_ref[f, 0]
            im = im + acc_ref[f, 1]
        out_ref[f, 0] = re.astype(out_ref.dtype)
        out_ref[f, 1] = im.astype(out_ref.dtype)


def term(turns, recv, send, press, acc=None, freqs=(0, 1), out_dtype=jnp.float32, tile=256):
    boxes, width = press.shape[2], press.shape[3]
    count = len(freqs)
    in_specs = [
        pl.BlockSpec(memory_space=pltpu.SMEM),
        pl.BlockSpec((tile, 8), lambda i: (i, 0)),
        pl.BlockSpec((8, boxes), lambda i: (0, 0)),
        pl.BlockSpec((count, 2, boxes, width), lambda i: (0, 0, 0, 0)),
    ]
    args = [turns, recv, send, press]
    if acc is not None:
        in_specs.append(pl.BlockSpec((count, 2, tile, width), lambda i: (0, 0, i, 0)))
        args.append(acc)
    return pl.pallas_call(
        functools.partial(term_body, freqs, acc is not None),
        grid=(boxes // tile,),
        in_specs=in_specs,
        out_specs=pl.BlockSpec((count, 2, tile, width), lambda i: (0, 0, i, 0)),
        out_shape=jax.ShapeDtypeStruct((count, 2, boxes, width), out_dtype),
        scratch_shapes=[pltpu.VMEM((1, count, 2, tile, boxes), jnp.bfloat16)],
        compiler_params=pltpu.CompilerParams(vmem_limit_bytes=48 * 1024 * 1024),
        cost_estimate=pl.CostEstimate(
            flops=count * 8 * boxes * boxes * width,
            bytes_accessed=12 * 1024 * 1024,
            transcendentals=0,
        ),
        input_output_aliases={4: 0} if acc is not None else {},
    )(*args)


def send_form(record):
    x, y, z, e, s, c = [record[i] for i in range(6)]
    return jnp.stack([x, y, z, e * e, 2.0 * e * s, 2.0 * e * c, e * s, e * c])


def recv_form(record):
    x, y, z, e, s, c = [record[i] for i in range(6)]
    return jnp.stack([x, y, z, s, c, s, s, s], axis=1)


def local(positions, spans, box_panel, panel_dihedral, freq_table, freq_index, pressures):
    panel_ids = jnp.arange(panel_dihedral.shape[0], dtype=jnp.int32)
    angle = jnp.sum(
        jnp.where(box_panel[:, None] == panel_ids[None, :], panel_dihedral[None, :], 0.0), axis=1
    )
    record = jnp.concatenate(
        [positions, spans[None, :], jnp.sin(angle)[None, :], jnp.cos(angle)[None, :]], axis=0
    )
    table_ids = jnp.arange(freq_table.shape[0], dtype=jnp.int32)
    waves = jnp.sum(
        jnp.where(freq_index[:, None] == table_ids[None, :], freq_table[None, :], 0.0), axis=1
    )
    turns = waves * (0.5 / jnp.pi)
    recv = recv_form(record)
    total = term(turns, recv, send_form(record), pressures)
    for distance in (1, 2, -1):
        rec = shifted(record, "wide", distance)
        press = shifted(pressures, "wide", distance)
        total = term(turns, recv, send_form(rec), press, total)
    return total


def solution(mesh):
    placed = (
        P(None, "wide"),
        P("wide"),
        P("wide"),
        P(),
        P(),
        P("groups"),
        P("groups", None, "wide", None),
    )
    return jax.shard_map(
        local,
        mesh=mesh,
        in_specs=placed,
        out_specs=P("groups", None, "wide", None),
        check_vma=False,
    )
```

profile of v0, /device:TPU:1, one launch (start us, length us, event | category | flops | bytes accessed | tf_op | source)
XLA Modules:
  0.0 132.1 jit_solution(10020746055426167269)
XLA Ops:
  0.0 2.6 %collective-permute-start.5 = (bf16[2,2,512,512]{3,2,1,0:T(8,128)(2,1)}, bf16[2,2,512,512]{3,2,1,0:T(8,128)(2,1)}, u32[]{:S(2)}, u32[]{:S(2)}) collective-permute-start(bf16[2,2,512,512]{3,2,1,0:T(8,128)(2,1)} %press_ref.1), channel_id=1, source_target_pairs={{15,0},{0,1},{1,2},{2,3},{3,4},{4,5},{5,6},{6,7},{7,8},{8,9},{9,10... | collective-permute-start | bytes 6291464 | tf_op jit(solution)/shard_map/ppermute | solution.py:26
  2.6 1.2 collective-permute-start.3
  3.9 0.0 collective-permute-start.1
  3.9 0.8 select_reduce_fusion
  4.7 0.7 pad_maximum_fusion
  5.4 1.8 %collective-permute-start.4 = (f32[6,512]{1,0:T(8,128)S(1)}, f32[6,512]{1,0:T(8,128)S(1)}, u32[]{:S(2)}, u32[]{:S(2)}) collective-permute-start(f32[6,512]{1,0:T(8,128)S(1)} %pad_maximum_fusion), channel_id=1, source_target_pairs={{15,0},{0,1},{1,2},{2,3},{3,4},{4,5},{5,6},{6,7},{7,8},{8,9},{9,10... | collective-permute-start | bytes 36872 | tf_op jit(solution)/shard_map/ppermute | solution.py:26
  7.2 2.1 %collective-permute-start.2 = (f32[6,512]{1,0:T(8,128)S(1)}, f32[6,512]{1,0:T(8,128)S(1)}, u32[]{:S(2)}, u32[]{:S(2)}) collective-permute-start(f32[6,512]{1,0:T(8,128)S(1)} %pad_maximum_fusion), channel_id=1, source_target_pairs={{14,0},{15,1},{0,2},{1,3},{2,4},{3,5},{4,6},{5,7},{6,8},{7,9},{8,1... | collective-permute-start | bytes 36872 | tf_op jit(solution)/shard_map/ppermute | solution.py:26
  9.4 0.8 slice_bitcast_fusion
  10.2 0.1 copy.26.recv_ref
  10.4 0.7 fusion.1
  11.1 0.7 stack.54.send_ref
  11.8 0.9 fusion
  12.6 0.0 copy-start
  12.6 1.6 %copy-done = bf16[2,2,512,512]{3,2,1,0:T(8,128)(2,1)S(1)} copy-done((bf16[2,2,512,512]{3,2,1,0:T(8,128)(2,1)S(1)}, bf16[2,2,512,512]{3,2,1,0:T(8,128)(2,1)}, u32[]{:S(2)}) %copy-start) | copy-done | bytes 2097176
  14.2 10.0 %shard_map.73.rest_0_ = f32[2,2,512,512]{3,2,1,0:T(8,128)} custom-call(f32[2]{0:T(128)S(1)} %broadcast_multiply_fusion.turns_ref, f32[512,8]{1,0:T(8,128)S(1)} %copy.26.recv_ref, f32[8,512]{1,0:T(8,128)S(1)} %stack.54.send_ref, bf16[2,2,512,512]{3,2,1,0:T(8,128)(2,1)S(1)} %copy-done), custom_call_target="tpu_custom_call" | custom-call | flops 2147483648 | bytes 12582912 | tf_op jit(solution)/shard_map/pallas_call | solution.py:94
  24.2 69.6 %collective-permute-done.4 = f32[6,512]{1,0:T(8,128)S(1)} collective-permute-done((f32[6,512]{1,0:T(8,128)S(1)}, f32[6,512]{1,0:T(8,128)S(1)}, u32[]{:S(2)}, u32[]{:S(2)}) %collective-permute-start.4) | collective-permute-done | bytes 12320 | tf_op jit(solution)/shard_map/ppermute | solution.py:26
  93.8 0.0 collective-permute-start
  93.8 0.2 collective-permute-done.2
  94.0 3.6 %collective-permute-done = f32[6,512]{1,0:T(8,128)S(1)} collective-permute-done((f32[6,512]{1,0:T(8,128)S(1)}, f32[6,512]{1,0:T(8,128)S(1)}, u32[]{:S(2)}, u32[]{:S(2)}) %collective-permute-start) | collective-permute-done | bytes 12320 | tf_op jit(solution)/shard_map/ppermute | solution.py:26
  97.7 0.0 collective-permute-done.5.press_ref
  97.7 11.7 %shard_map.74.rest_0_ = f32[2,2,512,512]{3,2,1,0:T(8,128)} custom-call(f32[2]{0:T(128)S(1)} %broadcast_multiply_fusion.turns_ref, f32[512,8]{1,0:T(8,128)S(1)} %copy.26.recv_ref, f32[8,512]{1,0:T(8,128)S(1)} %stack.23.send_ref, bf16[2,2,512,512]{3,2,1,0:T(8,128)(2,1)} %collective-permute-done.5.press_ref, ...), custom_call_target="tpu_custom_call", output_to_operand_aliasing={{}: (4, {})} | custom-call | flops 2147483648 | bytes 12582912 | tf_op jit(solution)/shard_map/pallas_call | solution.py:94
  109.4 0.0 collective-permute-done.3.press_ref
  109.4 11.7 %shard_map.75.rest_0_ = f32[2,2,512,512]{3,2,1,0:T(8,128)} custom-call(f32[2]{0:T(128)S(1)} %broadcast_multiply_fusion.turns_ref, f32[512,8]{1,0:T(8,128)S(1)} %copy.26.recv_ref, f32[8,512]{1,0:T(8,128)S(1)} %stack.22.send_ref, bf16[2,2,512,512]{3,2,1,0:T(8,128)(2,1)} %collective-permute-done.3.press_ref, ...), custom_call_target="tpu_custom_call", output_to_operand_aliasing={{}: (4, {})} | custom-call | flops 2147483648 | bytes 12582912 | tf_op jit(solution)/shard_map/pallas_call | solution.py:94
  121.1 0.0 collective-permute-done.1.press_ref
  121.1 11.0 %shard_map.76 = f32[2,2,512,512]{3,2,1,0:T(8,128)} custom-call(f32[2]{0:T(128)S(1)} %broadcast_multiply_fusion.turns_ref, f32[512,8]{1,0:T(8,128)S(1)} %copy.26.recv_ref, f32[8,512]{1,0:T(8,128)S(1)} %stack.21.send_ref, bf16[2,2,512,512]{3,2,1,0:T(8,128)(2,1)S(1)} %collective-permute-done.1.press_ref, ...), custom_call_target="tpu_custom_call", output_to_operand_aliasing={{}: (4, {})} | custom-call | flops 2147483648 | bytes 12582912 | tf_op jit(solution)/shard_map/pallas_call | solution.py:94
  (12 shorter events, 0.2 us)
Async XLA Ops:
  0.0 97.7 %collective-permute-start.5 = (bf16[2,2,512,512]{3,2,1,0:T(8,128)(2,1)}, bf16[2,2,512,512]{3,2,1,0:T(8,128)(2,1)}, u32[]{:S(2)}, u32[]{:S(2)}) collective-permute-start(bf16[2,2,512,512]{3,2,1,0:T(8,128)(2,1)} %press_ref.1), channel_id=1, source_target_pairs={{15,0},{0,1},{1,2},{2,3},{3,4},{4,5},{5,6},{6,7},{7,8},{8,9},{9,10... | collective-permute-start | bytes 6291464 | tf_op jit(solution)/shard_map/ppermute | solution.py:26
  2.6 106.8 %collective-permute-start.3 = (bf16[2,2,512,512]{3,2,1,0:T(8,128)(2,1)}, bf16[2,2,512,512]{3,2,1,0:T(8,128)(2,1)}, u32[]{:S(2)}, u32[]{:S(2)}) collective-permute-start(bf16[2,2,512,512]{3,2,1,0:T(8,128)(2,1)} %press_ref.1), channel_id=1, source_target_pairs={{14,0},{15,1},{0,2},{1,3},{2,4},{3,5},{4,6},{5,7},{6,8},{7,9},{8,1... | collective-permute-start | bytes 6291464 | tf_op jit(solution)/shard_map/ppermute | solution.py:26
  3.9 117.2 %collective-permute-start.1 = (bf16[2,2,512,512]{3,2,1,0:T(8,128)(2,1)}, bf16[2,2,512,512]{3,2,1,0:T(8,128)(2,1)S(1)}, u32[]{:S(2)}, u32[]{:S(2)}) collective-permute-start(bf16[2,2,512,512]{3,2,1,0:T(8,128)(2,1)} %press_ref.1), channel_id=1, source_target_pairs={{1,0},{2,1},{3,2},{4,3},{5,4},{6,5},{7,6},{8,7},{9,8},{10,9},{11,1... | collective-permute-start | bytes 6291464 | tf_op jit(solution)/shard_map/ppermute | solution.py:26
  5.4 88.3 %collective-permute-start.4 = (f32[6,512]{1,0:T(8,128)S(1)}, f32[6,512]{1,0:T(8,128)S(1)}, u32[]{:S(2)}, u32[]{:S(2)}) collective-permute-start(f32[6,512]{1,0:T(8,128)S(1)} %pad_maximum_fusion), channel_id=1, source_target_pairs={{15,0},{0,1},{1,2},{2,3},{3,4},{4,5},{5,6},{6,7},{7,8},{8,9},{9,10... | collective-permute-start | bytes 36872 | tf_op jit(solution)/shard_map/ppermute | solution.py:26
  7.2 86.7 %collective-permute-start.2 = (f32[6,512]{1,0:T(8,128)S(1)}, f32[6,512]{1,0:T(8,128)S(1)}, u32[]{:S(2)}, u32[]{:S(2)}) collective-permute-start(f32[6,512]{1,0:T(8,128)S(1)} %pad_maximum_fusion), channel_id=1, source_target_pairs={{14,0},{15,1},{0,2},{1,3},{2,4},{3,5},{4,6},{5,7},{6,8},{7,9},{8,1... | collective-permute-start | bytes 36872 | tf_op jit(solution)/shard_map/ppermute | solution.py:26
  12.6 1.6 %copy-start = (bf16[2,2,512,512]{3,2,1,0:T(8,128)(2,1)S(1)}, bf16[2,2,512,512]{3,2,1,0:T(8,128)(2,1)}, u32[]{:S(2)}) copy-start(bf16[2,2,512,512]{3,2,1,0:T(8,128)(2,1)} %press_ref.1) | copy-start | bytes 6291460
  93.8 3.9 %collective-permute-start = (f32[6,512]{1,0:T(8,128)S(1)}, f32[6,512]{1,0:T(8,128)S(1)}, u32[]{:S(2)}, u32[]{:S(2)}) collective-permute-start(f32[6,512]{1,0:T(8,128)S(1)} %pad_maximum_fusion), channel_id=1, source_target_pairs={{1,0},{2,1},{3,2},{4,3},{5,4},{6,5},{7,6},{8,7},{9,8},{10,9},{11,1... | collective-permute-start | bytes 36872 | tf_op jit(solution)/shard_map/ppermute | solution.py:26
where the time goes:
time: 133 us; the launch traced here: 132 us
  waiting for transfers between devices  73.4 us (55%)
  Pallas kernels  44.4 us (33%)
  starting transfers between devices  7.81 us (6%)
  local copies, waits for them, and re-layouts  3.44 us (3%)
  other arithmetic  3.1 us (2%)
    ppermute x6, waiting for transfers between devices, shifted(): lax.ppermute(block, axis, [((i - distance) % n, i) for i in range(n)])  73.4 us
    pallas_call x4, Pallas kernels, term(): pl.pallas_call(functools.partial(term_body, freqs, acc is not None), grid...  44.4 us
    ppermute x6, starting transfers between devices, shifted(): lax.ppermute(block, axis, [((i - distance) % n, i) for i in range(n)])  7.81 us
  transfers between devices with their start and end apart: 6, of which 3 were waited for; matrix products, arithmetic and copies ran while one was open for 4% of the time, Pallas kernels for 25%

commit v1 on v0

v1 whole, which is shorter than its diff:
```python
import functools

import jax
import jax.numpy as jnp
from jax import lax
from jax.experimental import pallas as pl
from jax.experimental.pallas import tpu as pltpu
from jax.sharding import PartitionSpec as P

SIN_COEF = (6.283182621002197, -41.3414192199707, 81.5961685180664, -76.5799560546875, 41.20474624633789, -12.27022647857666)
COS_COEF = (0.9999992251396179, -19.738981246948242, 64.9287109375, -85.27218627929688, 58.7929573059082, -21.074859619140625)
ROUNDER = 12582912.0
TURN = 0.15915494309189535
ROWS = 32
LANES = 128
RECORD = 32
VMEM = pl.BlockSpec(memory_space=pltpu.VMEM)
ANY = pl.BlockSpec(memory_space=pl.ANY)
PARAMS = pltpu.CompilerParams(vmem_limit_bytes=24 * 1024 * 1024)


def horner(v, coef):
    value = coef[-1] * v + coef[-2]
    for c in coef[-3::-1]:
        value = value * v + c
    return value


def cost(micros):
    return pl.CostEstimate(flops=micros << 32, bytes_accessed=1, transcendentals=0)


def prep_body(
    pos_any, span_any, panel_any, dihedral_any, table_any, index_any,
    send_ref, recv_ref, rows_ref,
    pos_ref, span_ref, panel_ref, dihedral_ref, table_ref, index_ref, sems
):
    boxes = pos_ref.shape[1]
    copies = [
        pltpu.make_async_copy(src, dst, sems.at[i])
        for i, (src, dst) in enumerate(
            [(pos_any, pos_ref), (span_any, span_ref), (panel_any, panel_ref)]
            + [(dihedral_any, dihedral_ref), (table_any, table_ref), (index_any, index_ref)]
        )
    ]
    for copy in copies:
        copy.start()
    for copy in copies:
        copy.wait()
    panel = panel_ref[...].reshape(1, boxes)
    angle = jnp.zeros(panel.shape, jnp.float32)
    for i in range(dihedral_ref.shape[0]):
        angle = jnp.where(panel == i, dihedral_ref[i], angle)
    sin, cos, span = jnp.sin(angle), jnp.cos(angle), span_ref[...].reshape(1, boxes)
    pos = pos_ref[...]
    send = jnp.concatenate(
        [pos, span * span, 2.0 * span * sin, 2.0 * span * cos, span * sin, span * cos], axis=0
    )
    send_ref[...] = send
    turns = [jnp.full_like(sin, table_ref[index_ref[f]] * TURN) for f in range(index_ref.shape[0])]
    recv_ref[...] = jnp.concatenate([pos, sin, cos, *turns, sin], axis=0).T
    high = send.astype(jnp.bfloat16).astype(jnp.float32)
    left = send - high
    middle = left.astype(jnp.bfloat16).astype(jnp.float32)
    rows_ref[...] = jnp.concatenate(
        [high, middle, left - middle, jnp.zeros_like(high)], axis=0
    ).astype(jnp.bfloat16)


def prepare(positions, spans, box_panel, panel_dihedral, freq_table, freq_index):
    args = (positions, spans, box_panel, panel_dihedral, freq_table, freq_index)
    boxes = spans.shape[0]
    return pl.pallas_call(
        prep_body,
        in_specs=[pl.BlockSpec(memory_space=pltpu.HBM)] * 6,
        out_specs=[VMEM] * 3,
        out_shape=[
            jax.ShapeDtypeStruct((8, boxes), jnp.float32),
            jax.ShapeDtypeStruct((boxes, 8), jnp.float32),
            jax.ShapeDtypeStruct((RECORD, boxes), jnp.bfloat16),
        ],
        scratch_shapes=[
            pltpu.VMEM(positions.shape, jnp.float32),
            pltpu.VMEM(spans.shape, jnp.float32),
            pltpu.VMEM(box_panel.shape, jnp.int32),
            pltpu.SMEM(panel_dihedral.shape, jnp.float32),
            pltpu.SMEM(freq_table.shape, jnp.float32),
            pltpu.SMEM(freq_index.shape, jnp.int32),
            pltpu.SemaphoreType.DMA((6,)),
        ],
        compiler_params=PARAMS,
        cost_estimate=cost(2),
    )(*[pltpu.with_memory_space_constraint(a, pltpu.HBM) for a in args])


def unpack(rows):
    parts = rows.astype(jnp.float32)
    return (parts[:8] + parts[8:16]) + parts[16:24]


def fill(recv_ref, send_ref, turns, stores):
    rows, boxes = recv_ref.shape[0], send_ref.shape[1]

    def row_block(i, carry):
        at = pl.ds(pl.multiple_of(i * ROWS, ROWS), ROWS)
        xi, yi, zi, si, ci = [
            jnp.broadcast_to(recv_ref[at, q : q + 1], (ROWS, LANES)) for q in range(5)
        ]
        for j in range(boxes // LANES):
            lanes = pl.ds(j * LANES, LANES)
            xj, yj, zj, e2, es2, ec2, es, ec = [send_ref[q : q + 1, lanes] for q in range(8)]
            dx, dy, dz = xi - xj, yi - yj, zi - zj
            rho = dy * dy + dz * dz + e2
            d2 = dx * dx + rho
            inv_d = lax.rsqrt(d2)
            inv = pl.reciprocal(rho, approx=True)
            inv = inv * (2.0 - rho * inv)
            normal_i = ci * dz - si * dy
            normal_j = ec2 * dz - es2 * dy
            planar = ci * ec + si * es
            amp = inv * (planar - normal_i * normal_j * inv) * (1.0 + dx * inv_d)
            lag = d2 * inv_d - dx
            for turn, (re, im) in zip(turns, stores):
                u = lag * turn
                u = u - ((u + ROUNDER) - ROUNDER)
                v = u * u
                re[at, lanes] = (amp * horner(v, COS_COEF)).astype(jnp.bfloat16)
                im[at, lanes] = (amp * u * horner(v, SIN_COEF)).astype(jnp.bfloat16)
        return carry

    lax.fori_loop(0, rows // ROWS, row_block, 0, unroll=4)


def dot(a, b):
    return jnp.dot(a, b, preferred_element_type=jnp.float32)


def product(kr, ks, pr, pi):
    return dot(kr, pr) + dot(ks, pi), dot(kr, pi) - dot(ks, pr)


def turns_of(recv_ref):
    return [recv_ref[:1, 5 + f : 6 + f] for f in range(2)]


def near_body(half, recv_ref, send0_ref, send1_ref, first_ref, second_ref, p1_ref, *rest):
    out_ref, k0_ref, k1_ref = rest[-3:]
    freqs = range(p1_ref.shape[0])
    tile, boxes = out_ref.shape[2], p1_ref.shape[2]
    turns = turns_of(recv_ref)
    recv = recv_ref.at[pl.ds(half * tile, tile)]
    fill(recv, send0_ref, turns, [(k0_ref.at[f, 0], k0_ref.at[f, 1]) for f in freqs])
    fill(recv, send1_ref, turns, [(k1_ref.at[f, 0], k1_ref.at[f, 1]) for f in freqs])
    for f, own_ref in enumerate((first_ref, second_ref)):
        re, im = own_ref[:boxes], own_ref[boxes : 2 * boxes]
        r0, i0 = product(k0_ref[f, 0], k0_ref[f, 1], re, im)
        r1, i1 = product(k1_ref[f, 0], k1_ref[f, 1], p1_ref[f, 0], p1_ref[f, 1])
        out_ref[f, 0] = r0 + r1
        out_ref[f, 1] = i0 + i1


def near(recv, send0, send1, first, second, p1, half, *after):
    freqs, _, boxes, width = p1.shape
    tile = boxes // 2
    return pl.pallas_call(
        functools.partial(near_body, half),
        in_specs=[VMEM] * 6 + [ANY] * len(after),
        out_specs=VMEM,
        out_shape=jax.ShapeDtypeStruct((freqs, 2, tile, width), jnp.float32),
        scratch_shapes=[pltpu.VMEM((freqs, 2, tile, boxes), jnp.bfloat16)] * 2,
        compiler_params=PARAMS,
        cost_estimate=cost(8),
    )(recv, send0, send1, first, second, p1, *after)


def choose(refs, rows):
    r = lax.rem(lax.axis_index("wide"), 4)
    inner = refs[1][rows]
    if len(refs) == 3:
        inner = jnp.where(r == 1, inner, refs[2][rows])
    return jnp.where(jnp.logical_or(r == 0, r == 3), refs[0][rows], inner)


def far_body(n_block, n_acc, recv_ref, *rest):
    block_refs, acc_refs = rest[:n_block], rest[n_block : n_block + n_acc]
    out_ref, later_ref, now_ref, p_ref, send_ref = rest[-5:]
    boxes = recv_ref.shape[0]
    p_ref[...] = choose(block_refs, slice(0, 2 * boxes))
    send_ref[...] = unpack(choose(block_refs, slice(2 * boxes, 2 * boxes + RECORD)))
    kern = [(now_ref.at[0], now_ref.at[1]), (later_ref.at[0], later_ref.at[1])]
    fill(recv_ref, send_ref, turns_of(recv_ref), kern)
    half = boxes // 2
    for h in range(2):
        rows = slice(h * half, h * half + half)
        re, im = product(now_ref[0, rows], now_ref[1, rows], p_ref[:boxes], p_ref[boxes:])
        if n_acc == 2:
            out_ref[0, rows] = acc_refs[h][0, 0] + re
            out_ref[1, rows] = acc_refs[h][0, 1] + im
        else:
            out_ref[0, 0, rows] = acc_refs[0][0, rows] + re
            out_ref[0, 1, rows] = acc_refs[0][1, rows] + im


def far(recv, block, accs, last):
    boxes, width = recv.shape[0], block[0].shape[1]
    if last:
        out = jax.ShapeDtypeStruct((2, 2, boxes, width), jnp.float32)
        spec = pl.BlockSpec((1, 2, boxes, width), lambda i: (0, 0, 0, 0))
    else:
        out, spec = jax.ShapeDtypeStruct((2, boxes, width), jnp.float32), VMEM
    return pl.pallas_call(
        functools.partial(far_body, len(block), len(accs)),
        grid=(1,),
        in_specs=[VMEM] * (1 + len(block) + len(accs)),
        out_specs=[spec, VMEM],
        out_shape=[out, jax.ShapeDtypeStruct((2, boxes, boxes), jnp.bfloat16)],
        scratch_shapes=[
            pltpu.VMEM((2, boxes, boxes), jnp.bfloat16),
            pltpu.VMEM((2 * boxes, width), jnp.bfloat16),
            pltpu.VMEM((8, boxes), jnp.float32),
        ],
        compiler_params=PARAMS,
        cost_estimate=cost(7),
    )(recv, *block, *accs)


def mid_body(n_block, kern_ref, *rest):
    block_refs = rest[:n_block]
    low_ref, high_ref, out_ref, p_ref = rest[n_block:]
    boxes = kern_ref.shape[1]
    p_ref[...] = choose(block_refs, slice(None))
    half = boxes // 2
    for h, acc_ref in enumerate((low_ref, high_ref)):
        rows = slice(h * half, h * half + half)
        re, im = product(kern_ref[0, rows], kern_ref[1, rows], p_ref[:boxes], p_ref[boxes:])
        out_ref[0, rows] = acc_ref[1, 0] + re
        out_ref[1, rows] = acc_ref[1, 1] + im


def mid(kern, block, low, high):
    boxes, width = kern.shape[1], block[0].shape[1]
    return pl.pallas_call(
        functools.partial(mid_body, len(block)),
        in_specs=[VMEM] * (3 + len(block)),
        out_specs=VMEM,
        out_shape=jax.ShapeDtypeStruct((2, boxes, width), jnp.float32),
        scratch_shapes=[pltpu.VMEM((2 * boxes, width), jnp.bfloat16)],
        compiler_params=PARAMS,
        cost_estimate=cost(2),
    )(kern, *block, low, high)


def end_body(kern_ref, x_ref, y_ref, acc_ref, whole_ref, out_ref, p_ref):
    boxes = p_ref.shape[0] // 2
    step = pl.program_id(0)
    tile = out_ref.shape[2]

    @pl.when(step == 0)
    def _():
        p_ref[...] = choose((x_ref, y_ref), slice(None))

    rows = pl.ds(pl.multiple_of(step * tile, tile), tile)
    re, im = product(kern_ref[0, rows], kern_ref[1, rows], p_ref[:boxes], p_ref[boxes:])
    out_ref[0, 0] = acc_ref[0, rows] + re
    out_ref[0, 1] = acc_ref[1, rows] + im


def end(kern, block, acc, out):
    boxes, width = kern.shape[1], block[0].shape[1]
    tile = boxes // 2
    return pl.pallas_call(
        end_body,
        grid=(2,),
        in_specs=[VMEM] * 4 + [ANY],
        out_specs=pl.BlockSpec((1, 2, tile, width), lambda i: (1, 0, i, 0)),
        out_shape=jax.ShapeDtypeStruct(out.shape, jnp.float32),
        scratch_shapes=[pltpu.VMEM((2 * boxes, width), jnp.bfloat16)],
        input_output_aliases={4: 0},
        compiler_params=PARAMS,
        cost_estimate=cost(2),
    )(kern, *block, acc, out)


def move(block, pairs):
    return lax.ppermute(block, "wide", pairs)


def routes(n):
    quads = range(0, n, 4)
    cross = [(b + r, b + (r ^ 2)) for b in quads for r in (0, 2)]
    cross += [(b + 3, (b + 7) % n) for b in quads] + [(b + 1, b + 1) for b in quads]
    spread = [
        p
        for b in quads
        for p in ((b + 1, b + 2), (b + 3, b + 1), (b, (b + 4) % n), ((b + 6) % n, b + 3))
    ]
    inner = [(b, b + 1) for b in quads]
    last = [p for b in quads for p in ((b + 1, b), (b + 2, b + 3))]
    pair = [(w, w ^ 1) for w in range(n)]
    return cross, spread, inner, last, pair


def ordered(value, *before):
    return lax.optimization_barrier((value, *before))[0]


def local(positions, spans, box_panel, panel_dihedral, freq_table, freq_index, pressures):
    n = lax.axis_size("wide")
    cross, spread, inner, last, pair = routes(n)
    _, _, boxes, width = pressures.shape
    send, recv, rows = prepare(
        positions, spans, box_panel, panel_dihedral, freq_table, freq_index
    )
    first = jnp.concatenate([pressures[0].reshape(2 * boxes, width), rows], axis=0)
    second = pressures[1].reshape(2 * boxes, width)
    crossed0 = move(first, cross)
    crossed1 = move(second, cross)
    beside = move(pressures, pair)
    send1 = move(send, pair)
    terms = functools.partial(near, recv, send, send1, first, second, beside)
    low = terms(0)
    high = terms(1)
    crossed0, crossed1, low, high = lax.optimization_barrier((crossed0, crossed1, low, high))
    spread0 = move(crossed0, spread)
    inner0 = move(crossed0, inner)
    spread1 = move(crossed1, spread)
    inner1 = move(crossed1, inner)
    last0 = move(spread0, last)
    total0, kern_a = far(recv, (spread0, inner0, crossed0), [low, high], False)
    out, kern_b = far(recv, (last0, spread0), [total0], True)
    spread1 = ordered(spread1, out)
    last1 = move(spread1, last)
    total1 = mid(kern_a, (spread1, inner1, crossed1), low, high)
    return end(kern_b, (last1, spread1), total1, out)


def solution(mesh):
    placed = (
        P(None, "wide"),
        P("wide"),
        P("wide"),
        P(),
        P(),
        P("groups"),
        P("groups", None, "wide", None),
    )
    return jax.shard_map(
        local,
        mesh=mesh,
        in_specs=placed,
        out_specs=P("groups", None, "wide", None),
        check_vma=False,
    )
```

time: 133 us -> 68.6 us (0.52)
  waiting for transfers between devices: 73.4 us -> 10.5 us
  starting transfers between devices: 7.81 us -> 28.8 us
  Pallas kernels: 44.4 us -> 28.2 us
  local copies, waits for them, and re-layouts: 3.44 us -> 0.14 us
  other arithmetic: 3.1 us -> 0.07 us
    ppermute x6 -> x10, waiting for transfers between devices: 73.4 us -> 10.5 us  [move(): return lax.ppermute(block, 'wide', pairs)]
    ppermute x6 -> x10, starting transfers between devices: 7.81 us -> 28.8 us  [move(): return lax.ppermute(block, 'wide', pairs)]
    pallas_call x4 -> x7, Pallas kernels: 44.4 us -> 28.2 us  [the longest x2 12 us: near(): pl.pallas_call(functools.partial(near_body, half), in_specs=[VMEM] * 6 +...]
    another operation x7 -> x0, local copies, waits for them, and re-layouts: 1.8 us -> none  [the longest x3 0.98 us: recv_form(): return jnp.stack([x, y, z, s, c, s, s, s], axis=1)]
    reduce_sum x2 -> x0, other arithmetic: 1.64 us -> none  [the longest x1 0.85 us: local(): jnp.sum(jnp.where(freq_index[:, None] == table_ids[None, :], freq_table[N...]
    unnamed x2, local copies, waits for them, and re-layouts: 1.59 us -> 0.01 us
  transfers between devices with their start and end apart: 6 -> 10, of which waited for: 3 -> 4; matrix products, arithmetic and copies ran while one was open for 4% -> 0% of each run, Pallas kernels for 25% -> 38%
where the time goes in v1:
time: 68.6 us; the launch traced here: 68 us
  starting transfers between devices  28.8 us (42%)
  Pallas kernels  28.2 us (41%)
  waiting for transfers between devices  10.5 us (15%)
    ppermute x10, starting transfers between devices, move(): return lax.ppermute(block, 'wide', pairs)  28.8 us
    pallas_call x2, Pallas kernels, near(): pl.pallas_call(functools.partial(near_body, half), in_specs=[VMEM] * 6 +...  12 us
    pallas_call x2, Pallas kernels, far(): pl.pallas_call(functools.partial(far_body, len(block), len(accs)), grid=(...  11.3 us
    ppermute x10, waiting for transfers between devices, move(): return lax.ppermute(block, 'wide', pairs)  10.5 us
    pallas_call x1, Pallas kernels, end(): pl.pallas_call(end_body, grid=(2,), in_specs=[VMEM] * 4 + [ANY], out_spec...  2.52 us
  transfers between devices with their start and end apart: 10, of which 4 were waited for; matrix products, arithmetic and copies ran while one was open for 0% of the time, Pallas kernels for 38%

profile of v1, /device:TPU:1, one launch (start us, length us, event | category | flops | bytes accessed | tf_op | source)
XLA Modules:
  0.0 68.0 jit_solution(9809192581253182998)
XLA Ops:
  0.0 0.0 copy-start
  0.0 0.1 collective-permute-start.3
  0.1 1.1 %shard_map.73 = (f32[8,512]{1,0:T(8,128)S(1)}, f32[512,8]{1,0:T(8,128)S(1)}, bf16[32,512]{1,0:T(8,128)(2,1)S(1)}) custom-call(f32[3,512]{1,0:T(4,128)} %pos_any.1, f32[512]{0:T(512)} %span_any.1, s32[512]{0:T(512)} %panel_any.1, f32[64]{0:T(128)} %dihedral_any.1, f32[16]{0:T(128)} %table_any.1, s32[2]{0:T(128)} %index_any.1), custom_call_target="tpu_custom_call" | custom-call | flops 8589934592 | bytes 1 | tf_op jit(solution)/shard_map/pallas_call | solution.py:73
  1.2 0.6 collective-permute-start.2
  1.8 0.0 copy-done
  1.8 0.1 fusion
  1.9 0.1 pad_maximum_fusion.first_ref
  2.0 0.7 %collective-permute-start = (bf16[1056,512]{1,0:T(8,128)(2,1)S(1)}, bf16[1056,512]{1,0:T(8,128)(2,1)S(1)}, u32[]{:S(2)}, u32[]{:S(2)}) collective-permute-start(bf16[1056,512]{1,0:T(8,128)(2,1)S(1)} %pad_maximum_fusion.first_ref), channel_id=1, source_target_pairs={{0,2},{2,0},{4,6},{6,4},{8,10},{10,8},{12,14},{14,12},{3,7},{7,11}... | collective-permute-start | bytes 3244040 | tf_op jit(solution)/shard_map/ppermute | solution.py:285
  2.7 0.7 %collective-permute-start.1 = (bf16[1024,512]{1,0:T(8,128)(2,1)S(1)}, bf16[1024,512]{1,0:T(8,128)(2,1)S(1)}, u32[]{:S(2)}, u32[]{:S(2)}) collective-permute-start(bf16[1024,512]{1,0:T(8,128)(2,1)S(1)} %bitcast.2), channel_id=1, source_target_pairs={{0,2},{2,0},{4,6},{6,4},{8,10},{10,8},{12,14},{14,12},{3,7},{7,11}... | collective-permute-start | bytes 3145736 | tf_op jit(solution)/shard_map/ppermute | solution.py:285
  3.5 0.7 %collective-permute-done.2.send1_ref = f32[8,512]{1,0:T(8,128)S(1)} collective-permute-done((f32[8,512]{1,0:T(8,128)S(1)}, f32[8,512]{1,0:T(8,128)S(1)}, u32[]{:S(2)}, u32[]{:S(2)}) %collective-permute-start.2) | collective-permute-done | bytes 16416 | tf_op jit(solution)/shard_map/ppermute | solution.py:285
  4.2 0.2 collective-permute-done.3.p1_ref
  4.4 6.0 %shard_map.75.rest_4_ = f32[2,2,256,512]{3,2,1,0:T(8,128)S(1)} custom-call(f32[512,8]{1,0:T(8,128)S(1)} %get-tuple-element.17.recv_ref, f32[8,512]{1,0:T(8,128)S(1)} %get-tuple-element.19.send0_ref, f32[8,512]{1,0:T(8,128)S(1)} %collective-permute-done.2.send1_ref, bf16[1056,512]{1,0:T(8,128)(2,1)S(1)} %pad_maximum_fusion.first_ref, ...), custom_call_target="tpu_custom_call" | custom-call | flops 34359738368 | bytes 1 | tf_op jit(solution)/shard_map/pallas_call | solution.py:165
  10.4 6.0 %shard_map.74.rest_3_ = f32[2,2,256,512]{3,2,1,0:T(8,128)S(1)} custom-call(f32[512,8]{1,0:T(8,128)S(1)} %get-tuple-element.17.recv_ref, f32[8,512]{1,0:T(8,128)S(1)} %get-tuple-element.19.send0_ref, f32[8,512]{1,0:T(8,128)S(1)} %collective-permute-done.2.send1_ref, bf16[1056,512]{1,0:T(8,128)(2,1)S(1)} %pad_maximum_fusion.first_ref, ...), custom_call_target="tpu_custom_call" | custom-call | flops 34359738368 | bytes 1 | tf_op jit(solution)/shard_map/pallas_call | solution.py:165
  16.4 0.0 collective-permute-done.1.rest_2_
  16.4 0.0 collective-permute-done.rest_2_
  16.4 16.4 %collective-permute-start.4 = (bf16[1056,512]{1,0:T(8,128)(2,1)S(1)}, bf16[1056,512]{1,0:T(8,128)(2,1)S(1)}, u32[]{:S(2)}, u32[]{:S(2)}) collective-permute-start(bf16[1056,512]{1,0:T(8,128)(2,1)S(1)} %collective-permute-done.rest_2_), channel_id=1, source_target_pairs={{1,2},{3,1},{0,4},{6,3},{5,6},{7,5},{4,8},{10,7},{9,10},{11,9},{8,... | collective-permute-start | bytes 3244040 | tf_op jit(solution)/shard_map/ppermute | solution.py:285
  32.8 1.3 %collective-permute-start.6 = (bf16[1056,512]{1,0:T(8,128)(2,1)S(1)}, bf16[1056,512]{1,0:T(8,128)(2,1)S(1)}, u32[]{:S(2)}, u32[]{:S(2)}) collective-permute-start(bf16[1056,512]{1,0:T(8,128)(2,1)S(1)} %collective-permute-done.rest_2_), channel_id=1, source_target_pairs={{0,1},{4,5},{8,9},{12,13},{16,17},{20,21},{24,25},{28,29}} | collective-permute-start | bytes 3244040 | tf_op jit(solution)/shard_map/ppermute | solution.py:285
  34.1 1.9 %collective-permute-start.7 = (bf16[1024,512]{1,0:T(8,128)(2,1)S(1)}, bf16[1024,512]{1,0:T(8,128)(2,1)S(1)}, u32[]{:S(2)}, u32[]{:S(2)}) collective-permute-start(bf16[1024,512]{1,0:T(8,128)(2,1)S(1)} %collective-permute-done.1.rest_2_), channel_id=1, source_target_pairs={{1,2},{3,1},{0,4},{6,3},{5,6},{7,5},{4,8},{10,7},{9,10},{11,9},{8,... | collective-permute-start | bytes 3145736 | tf_op jit(solution)/shard_map/ppermute | solution.py:285
  36.0 1.3 %collective-permute-start.9 = (bf16[1024,512]{1,0:T(8,128)(2,1)S(1)}, bf16[1024,512]{1,0:T(8,128)(2,1)S(1)}, u32[]{:S(2)}, u32[]{:S(2)}) collective-permute-start(bf16[1024,512]{1,0:T(8,128)(2,1)S(1)} %collective-permute-done.1.rest_2_), channel_id=1, source_target_pairs={{0,1},{4,5},{8,9},{12,13},{16,17},{20,21},{24,25},{28,29}} | collective-permute-start | bytes 3145736 | tf_op jit(solution)/shard_map/ppermute | solution.py:285
  37.3 8.7 %collective-permute-done.4.rest_0_.rest_1_ = bf16[1056,512]{1,0:T(8,128)(2,1)S(1)} collective-permute-done((bf16[1056,512]{1,0:T(8,128)(2,1)S(1)}, bf16[1056,512]{1,0:T(8,128)(2,1)S(1)}, u32[]{:S(2)}, u32[]{:S(2)}) %collective-permute-start.4) | collective-permute-done | bytes 1081376 | tf_op jit(solution)/shard_map/ppermute | solution.py:285
  46.0 4.5 %collective-permute-start.5 = (bf16[1056,512]{1,0:T(8,128)(2,1)S(1)}, bf16[1056,512]{1,0:T(8,128)(2,1)S(1)}, u32[]{:S(2)}, u32[]{:S(2)}) collective-permute-start(bf16[1056,512]{1,0:T(8,128)(2,1)S(1)} %collective-permute-done.4.rest_0_.rest_1_), channel_id=1, source_target_pairs={{1,0},{2,3},{5,4},{6,7},{9,8},{10,11},{13,12},{14,15},{17,16},{18,... | collective-permute-start | bytes 3244040 | tf_op jit(solution)/shard_map/ppermute | solution.py:285
  50.6 0.0 collective-permute-done.6.rest_1_
  50.6 5.0 %shard_map.76 = (f32[2,512,512]{2,1,0:T(8,128)S(1)}, bf16[2,512,512]{2,1,0:T(8,128)(2,1)S(1)}) custom-call(f32[512,8]{1,0:T(8,128)S(1)} %get-tuple-element.17.recv_ref, bf16[1056,512]{1,0:T(8,128)(2,1)S(1)} %collective-permute-done.4.rest_0_.rest_1_, bf16[1056,512]{1,0:T(8,128)(2,1)S(1)} %collective-permute-done.6.rest_1_, ...), custom_call_target="tpu_custom_call" | custom-call | flops 30064771072 | bytes 1 | tf_op jit(solution)/shard_map/pallas_call | solution.py:211
  55.6 0.0 collective-permute-done.5.rest_0_
  55.6 6.3 %shard_map.77 = (f32[2,2,512,512]{3,2,1,0:T(8,128)}, bf16[2,512,512]{2,1,0:T(8,128)(2,1)S(1)}) custom-call(f32[512,8]{1,0:T(8,128)S(1)} %get-tuple-element.17.recv_ref, bf16[1056,512]{1,0:T(8,128)(2,1)S(1)} %collective-permute-done.5.rest_0_, bf16[1056,512]{1,0:T(8,128)(2,1)S(1)} %collective-permute-done.4.rest_0_.rest_1_, ...), custom_call_target="tpu_custom_call" | custom-call | flops 30064771072 | bytes 1 | tf_op jit(solution)/shard_map/pallas_call | solution.py:211
  61.9 0.0 collective-permute-done.7.rest_0_.y_ref
  61.9 1.3 %collective-permute-start.8 = (bf16[1024,512]{1,0:T(8,128)(2,1)S(1)}, bf16[1024,512]{1,0:T(8,128)(2,1)S(1)}, u32[]{:S(2)}, u32[]{:S(2)}) collective-permute-start(bf16[1024,512]{1,0:T(8,128)(2,1)S(1)} %collective-permute-done.7.rest_0_.y_ref), channel_id=1, source_target_pairs={{1,0},{2,3},{5,4},{6,7},{9,8},{10,11},{13,12},{14,15},{17,16},{18,... | collective-permute-start | bytes 3145736 | tf_op jit(solution)/shard_map/ppermute | solution.py:285
  63.3 0.0 collective-permute-done.9.rest_1_
  63.3 1.3 %shard_map.78.acc_ref = f32[2,512,512]{2,1,0:T(8,128)S(1)} custom-call(bf16[2,512,512]{2,1,0:T(8,128)(2,1)S(1)} %get-tuple-element.28.kern_ref, bf16[1024,512]{1,0:T(8,128)(2,1)S(1)} %collective-permute-done.7.rest_0_.y_ref, bf16[1024,512]{1,0:T(8,128)(2,1)S(1)} %collective-permute-done.9.rest_1_, bf16[1024,512]{1,0:T(8,128)(2,1)S(1)} %collective-permute-done.1.rest_2_, ...), custom_call_target="tpu_custom_call" | custom-call | flops 8589934592 | bytes 1 | tf_op jit(solution)/shard_map/pallas_call | solution.py:242
  64.6 0.9 %collective-permute-done.8.x_ref = bf16[1024,512]{1,0:T(8,128)(2,1)S(1)} collective-permute-done((bf16[1024,512]{1,0:T(8,128)(2,1)S(1)}, bf16[1024,512]{1,0:T(8,128)(2,1)S(1)}, u32[]{:S(2)}, u32[]{:S(2)}) %collective-permute-start.8) | collective-permute-done | bytes 1048608 | tf_op jit(solution)/shard_map/ppermute | solution.py:285
  65.5 2.5 %shard_map.79 = f32[2,2,512,512]{3,2,1,0:T(8,128)} custom-call(bf16[2,512,512]{2,1,0:T(8,128)(2,1)S(1)} %get-tuple-element.24.kern_ref, bf16[1024,512]{1,0:T(8,128)(2,1)S(1)} %collective-permute-done.8.x_ref, bf16[1024,512]{1,0:T(8,128)(2,1)S(1)} %collective-permute-done.7.rest_0_.y_ref, ...), custom_call_target="tpu_custom_call", output_to_operand_aliasing={{}: (4, {})} | custom-call | flops 8589934592 | bytes 1 | tf_op jit(solution)/shard_map/pallas_call | solution.py:271
Async XLA Ops:
  0.0 1.8 %copy-start = (bf16[2,2,512,512]{3,2,1,0:T(8,128)(2,1)S(1)}, bf16[2,2,512,512]{3,2,1,0:T(8,128)(2,1)}, u32[]{:S(2)}) copy-start(bf16[2,2,512,512]{3,2,1,0:T(8,128)(2,1)} %param.13) | copy-start | bytes 6291460
  0.0 4.4 %collective-permute-start.3 = (bf16[2,2,512,512]{3,2,1,0:T(8,128)(2,1)}, bf16[2,2,512,512]{3,2,1,0:T(8,128)(2,1)S(1)}, u32[]{:S(2)}, u32[]{:S(2)}) collective-permute-start(bf16[2,2,512,512]{3,2,1,0:T(8,128)(2,1)} %param.13), channel_id=1, source_target_pairs={{0,1},{1,0},{2,3},{3,2},{4,5},{5,4},{6,7},{7,6},{8,9},{9,8},{10,11... | collective-permute-start | bytes 6291464 | tf_op jit(solution)/shard_map/ppermute | solution.py:285
  1.2 3.0 %collective-permute-start.2 = (f32[8,512]{1,0:T(8,128)S(1)}, f32[8,512]{1,0:T(8,128)S(1)}, u32[]{:S(2)}, u32[]{:S(2)}) collective-permute-start(f32[8,512]{1,0:T(8,128)S(1)} %get-tuple-element.19.send0_ref), channel_id=1, source_target_pairs={{0,1},{1,0},{2,3},{3,2},{4,5},{5,4},{6,7},{7,6},{8,9},{9,8},{10,11... | collective-permute-start | bytes 49160 | tf_op jit(solution)/shard_map/ppermute | solution.py:285
  2.0 14.4 %collective-permute-start = (bf16[1056,512]{1,0:T(8,128)(2,1)S(1)}, bf16[1056,512]{1,0:T(8,128)(2,1)S(1)}, u32[]{:S(2)}, u32[]{:S(2)}) collective-permute-start(bf16[1056,512]{1,0:T(8,128)(2,1)S(1)} %pad_maximum_fusion.first_ref), channel_id=1, source_target_pairs={{0,2},{2,0},{4,6},{6,4},{8,10},{10,8},{12,14},{14,12},{3,7},{7,11}... | collective-permute-start | bytes 3244040 | tf_op jit(solution)/shard_map/ppermute | solution.py:285
  2.7 13.6 %collective-permute-start.1 = (bf16[1024,512]{1,0:T(8,128)(2,1)S(1)}, bf16[1024,512]{1,0:T(8,128)(2,1)S(1)}, u32[]{:S(2)}, u32[]{:S(2)}) collective-permute-start(bf16[1024,512]{1,0:T(8,128)(2,1)S(1)} %bitcast.2), channel_id=1, source_target_pairs={{0,2},{2,0},{4,6},{6,4},{8,10},{10,8},{12,14},{14,12},{3,7},{7,11}... | collective-permute-start | bytes 3145736 | tf_op jit(solution)/shard_map/ppermute | solution.py:285
  16.4 29.7 %collective-permute-start.4 = (bf16[1056,512]{1,0:T(8,128)(2,1)S(1)}, bf16[1056,512]{1,0:T(8,128)(2,1)S(1)}, u32[]{:S(2)}, u32[]{:S(2)}) collective-permute-start(bf16[1056,512]{1,0:T(8,128)(2,1)S(1)} %collective-permute-done.rest_2_), channel_id=1, source_target_pairs={{1,2},{3,1},{0,4},{6,3},{5,6},{7,5},{4,8},{10,7},{9,10},{11,9},{8,... | collective-permute-start | bytes 3244040 | tf_op jit(solution)/shard_map/ppermute | solution.py:285
  32.8 17.8 %collective-permute-start.6 = (bf16[1056,512]{1,0:T(8,128)(2,1)S(1)}, bf16[1056,512]{1,0:T(8,128)(2,1)S(1)}, u32[]{:S(2)}, u32[]{:S(2)}) collective-permute-start(bf16[1056,512]{1,0:T(8,128)(2,1)S(1)} %collective-permute-done.rest_2_), channel_id=1, source_target_pairs={{0,1},{4,5},{8,9},{12,13},{16,17},{20,21},{24,25},{28,29}} | collective-permute-start | bytes 3244040 | tf_op jit(solution)/shard_map/ppermute | solution.py:285
  34.1 27.8 %collective-permute-start.7 = (bf16[1024,512]{1,0:T(8,128)(2,1)S(1)}, bf16[1024,512]{1,0:T(8,128)(2,1)S(1)}, u32[]{:S(2)}, u32[]{:S(2)}) collective-permute-start(bf16[1024,512]{1,0:T(8,128)(2,1)S(1)} %collective-permute-done.1.rest_2_), channel_id=1, source_target_pairs={{1,2},{3,1},{0,4},{6,3},{5,6},{7,5},{4,8},{10,7},{9,10},{11,9},{8,... | collective-permute-start | bytes 3145736 | tf_op jit(solution)/shard_map/ppermute | solution.py:285
  36.0 27.2 %collective-permute-start.9 = (bf16[1024,512]{1,0:T(8,128)(2,1)S(1)}, bf16[1024,512]{1,0:T(8,128)(2,1)S(1)}, u32[]{:S(2)}, u32[]{:S(2)}) collective-permute-start(bf16[1024,512]{1,0:T(8,128)(2,1)S(1)} %collective-permute-done.1.rest_2_), channel_id=1, source_target_pairs={{0,1},{4,5},{8,9},{12,13},{16,17},{20,21},{24,25},{28,29}} | collective-permute-start | bytes 3145736 | tf_op jit(solution)/shard_map/ppermute | solution.py:285
  46.0 9.6 %collective-permute-start.5 = (bf16[1056,512]{1,0:T(8,128)(2,1)S(1)}, bf16[1056,512]{1,0:T(8,128)(2,1)S(1)}, u32[]{:S(2)}, u32[]{:S(2)}) collective-permute-start(bf16[1056,512]{1,0:T(8,128)(2,1)S(1)} %collective-permute-done.4.rest_0_.rest_1_), channel_id=1, source_target_pairs={{1,0},{2,3},{5,4},{6,7},{9,8},{10,11},{13,12},{14,15},{17,16},{18,... | collective-permute-start | bytes 3244040 | tf_op jit(solution)/shard_map/ppermute | solution.py:285
  61.9 3.6 %collective-permute-start.8 = (bf16[1024,512]{1,0:T(8,128)(2,1)S(1)}, bf16[1024,512]{1,0:T(8,128)(2,1)S(1)}, u32[]{:S(2)}, u32[]{:S(2)}) collective-permute-start(bf16[1024,512]{1,0:T(8,128)(2,1)S(1)} %collective-permute-done.7.rest_0_.y_ref), channel_id=1, source_target_pairs={{1,0},{2,3},{5,4},{6,7},{9,8},{10,11},{13,12},{14,15},{17,16},{18,... | collective-permute-start | bytes 3145736 | tf_op jit(solution)/shard_map/ppermute | solution.py:285

commit v2 on v1

--- a/solution.py
+++ b/solution.py
@@ -27,7 +27,7 @@
 
 
 def cost(micros):
-    return pl.CostEstimate(flops=micros << 32, bytes_accessed=1, transcendentals=0)
+    return pl.CostEstimate(flops=micros << 33, bytes_accessed=1, transcendentals=0)
 
 
 def prep_body(
@@ -143,34 +143,32 @@
     return [recv_ref[:1, 5 + f : 6 + f] for f in range(2)]
 
 
-def near_body(half, recv_ref, send0_ref, send1_ref, first_ref, second_ref, p1_ref, *rest):
-    out_ref, k0_ref, k1_ref = rest[-3:]
-    freqs = range(p1_ref.shape[0])
-    tile, boxes = out_ref.shape[2], p1_ref.shape[2]
+def near_body(recv_ref, send0_ref, send1_ref, p0_ref, p1_ref, out_ref, k0_ref, k1_ref):
+    freqs = range(p0_ref.shape[0])
+    half = recv_ref.shape[0] // 2
     turns = turns_of(recv_ref)
-    recv = recv_ref.at[pl.ds(half * tile, tile)]
-    fill(recv, send0_ref, turns, [(k0_ref.at[f, 0], k0_ref.at[f, 1]) for f in freqs])
-    fill(recv, send1_ref, turns, [(k1_ref.at[f, 0], k1_ref.at[f, 1]) for f in freqs])
-    for f, own_ref in enumerate((first_ref, second_ref)):
-        re, im = own_ref[:boxes], own_ref[boxes : 2 * boxes]
-        r0, i0 = product(k0_ref[f, 0], k0_ref[f, 1], re, im)
-        r1, i1 = product(k1_ref[f, 0], k1_ref[f, 1], p1_ref[f, 0], p1_ref[f, 1])
-        out_ref[f, 0] = r0 + r1
-        out_ref[f, 1] = i0 + i1
-
-
-def near(recv, send0, send1, first, second, p1, half, *after):
-    freqs, _, boxes, width = p1.shape
-    tile = boxes // 2
-    return pl.pallas_call(
-        functools.partial(near_body, half),
-        in_specs=[VMEM] * 6 + [ANY] * len(after),
+    fill(recv_ref, send0_ref, turns, [(k0_ref.at[f, 0], k0_ref.at[f, 1]) for f in freqs])
+    fill(recv_ref, send1_ref, turns, [(k1_ref.at[f, 0], k1_ref.at[f, 1]) for f in freqs])
+    for f in freqs:
+        for h in range(2):
+            rows = slice(h * half, h * half + half)
+            r0, i0 = product(k0_ref[f, 0, rows], k0_ref[f, 1, rows], p0_ref[f, 0], p0_ref[f, 1])
+            r1, i1 = product(k1_ref[f, 0, rows], k1_ref[f, 1, rows], p1_ref[f, 0], p1_ref[f, 1])
+            out_ref[f, 0, rows] = r0 + r1
+            out_ref[f, 1, rows] = i0 + i1
+
+
+def near(recv, send0, send1, p0, p1):
+    freqs, _, boxes, width = p0.shape
+    return pl.pallas_call(
+        near_body,
+        in_specs=[VMEM] * 5,
         out_specs=VMEM,
-        out_shape=jax.ShapeDtypeStruct((freqs, 2, tile, width), jnp.float32),
-        scratch_shapes=[pltpu.VMEM((freqs, 2, tile, boxes), jnp.bfloat16)] * 2,
-        compiler_params=PARAMS,
-        cost_estimate=cost(8),
-    )(recv, send0, send1, first, second, p1, *after)
+        out_shape=jax.ShapeDtypeStruct((freqs, 2, boxes, width), jnp.float32),
+        scratch_shapes=[pltpu.VMEM((freqs, 2, boxes, boxes), jnp.bfloat16)] * 2,
+        compiler_params=PARAMS,
+        cost_estimate=cost(12),
+    )(recv, send0, send1, p0, p1)
 
 
 def choose(refs, rows):
@@ -181,77 +179,82 @@
     return jnp.where(jnp.logical_or(r == 0, r == 3), refs[0][rows], inner)
 
 
-def far_body(n_block, n_acc, recv_ref, *rest):
-    block_refs, acc_refs = rest[:n_block], rest[n_block : n_block + n_acc]
-    out_ref, later_ref, now_ref, p_ref, send_ref = rest[-5:]
+def build_body(n_block, recv_ref, *rest):
+    block_refs, kern_ref, send_ref = rest[:n_block], rest[-2], rest[-1]
     boxes = recv_ref.shape[0]
-    p_ref[...] = choose(block_refs, slice(0, 2 * boxes))
-    send_ref[...] = unpack(choose(block_refs, slice(2 * boxes, 2 * boxes + RECORD)))
-    kern = [(now_ref.at[0], now_ref.at[1]), (later_ref.at[0], later_ref.at[1])]
-    fill(recv_ref, send_ref, turns_of(recv_ref), kern)
+    send_ref[...] = unpack(choose(block_refs, slice(boxes, boxes + RECORD)))
+    stores = [(kern_ref.at[f, 0], kern_ref.at[f, 1]) for f in range(kern_ref.shape[0])]
+    fill(recv_ref, send_ref, turns_of(recv_ref), stores)
+
+
+def build(recv, block, *after):
+    boxes = recv.shape[0]
+    return pl.pallas_call(
+        functools.partial(build_body, len(block)),
+        in_specs=[VMEM] * (1 + len(block)) + [ANY] * len(after),
+        out_specs=VMEM,
+        out_shape=jax.ShapeDtypeStruct((2, 2, boxes, boxes), jnp.bfloat16),
+        scratch_shapes=[pltpu.VMEM((8, boxes), jnp.float32)],
+        compiler_params=PARAMS,
+        cost_estimate=cost(4),
+    )(recv, *block, *after)
+
+
+def part(kern_ref, f, p, which, rows):
+    kr, ks = kern_ref[f, 0, rows], kern_ref[f, 1, rows]
+    if which == 0:
+        return dot(kr, p), -dot(ks, p)
+    if which == 1:
+        return dot(ks, p), dot(kr, p)
+    boxes = p.shape[0] // 2
+    return product(kr, ks, p[:boxes], p[boxes:])
+
+
+def fold_body(f, which, n_blocks, n_acc, *refs):
+    kern_refs, refs = refs[: len(n_blocks)], refs[len(n_blocks) :]
+    blocks = []
+    for n in n_blocks:
+        blocks.append(refs[:n])
+        refs = refs[n:]
+    acc_refs, (out_ref, *p_refs) = refs[:n_acc], refs[-1 - len(n_blocks) :]
+    boxes = kern_refs[0].shape[2]
+    out = out_ref.at[0] if len(out_ref.shape) == 4 else out_ref
+    for block, p_ref in zip(blocks, p_refs):
+        p_ref[...] = choose(block, slice(0, p_ref.shape[0]))
     half = boxes // 2
     for h in range(2):
         rows = slice(h * half, h * half + half)
-        re, im = product(now_ref[0, rows], now_ref[1, rows], p_ref[:boxes], p_ref[boxes:])
-        if n_acc == 2:
-            out_ref[0, rows] = acc_refs[h][0, 0] + re
-            out_ref[1, rows] = acc_refs[h][0, 1] + im
-        else:
-            out_ref[0, 0, rows] = acc_refs[0][0, rows] + re
-            out_ref[0, 1, rows] = acc_refs[0][1, rows] + im
-
-
-def far(recv, block, accs, last):
-    boxes, width = recv.shape[0], block[0].shape[1]
-    if last:
+        acc = acc_refs[0].at[f] if len(acc_refs[0].shape) == 4 else acc_refs[0]
+        re, im = acc[0, rows], acc[1, rows]
+        for kern_ref, p_ref in zip(kern_refs, p_refs):
+            more_re, more_im = part(kern_ref, f, p_ref[...], which, rows)
+            re, im = re + more_re, im + more_im
+        out[0, rows] = re
+        out[1, rows] = im
+
+
+def fold(f, which, kerns, blocks, accs, final=False):
+    boxes, width = kerns[0].shape[2], blocks[0][0].shape[1]
+    depth = boxes * (2 if which == 2 else 1)
+    if final:
         out = jax.ShapeDtypeStruct((2, 2, boxes, width), jnp.float32)
-        spec = pl.BlockSpec((1, 2, boxes, width), lambda i: (0, 0, 0, 0))
+        spec = pl.BlockSpec((1, 2, boxes, width), lambda i: (f, 0, 0, 0))
     else:
         out, spec = jax.ShapeDtypeStruct((2, boxes, width), jnp.float32), VMEM
-    return pl.pallas_call(
-        functools.partial(far_body, len(block), len(accs)),
+    args = [*kerns, *[r for block in blocks for r in block], *accs]
+    return pl.pallas_call(
+        functools.partial(fold_body, f, which, [len(b) for b in blocks], len(accs)),
         grid=(1,),
-        in_specs=[VMEM] * (1 + len(block) + len(accs)),
-        out_specs=[spec, VMEM],
-        out_shape=[out, jax.ShapeDtypeStruct((2, boxes, boxes), jnp.bfloat16)],
-        scratch_shapes=[
-            pltpu.VMEM((2, boxes, boxes), jnp.bfloat16),
-            pltpu.VMEM((2 * boxes, width), jnp.bfloat16),
-            pltpu.VMEM((8, boxes), jnp.float32),
-        ],
-        compiler_params=PARAMS,
-        cost_estimate=cost(7),
-    )(recv, *block, *accs)
-
-
-def mid_body(n_block, kern_ref, *rest):
-    block_refs = rest[:n_block]
-    low_ref, high_ref, out_ref, p_ref = rest[n_block:]
-    boxes = kern_ref.shape[1]
-    p_ref[...] = choose(block_refs, slice(None))
-    half = boxes // 2
-    for h, acc_ref in enumerate((low_ref, high_ref)):
-        rows = slice(h * half, h * half + half)
-        re, im = product(kern_ref[0, rows], kern_ref[1, rows], p_ref[:boxes], p_ref[boxes:])
-        out_ref[0, rows] = acc_ref[1, 0] + re
-        out_ref[1, rows] = acc_ref[1, 1] + im
-
-
-def mid(kern, block, low, high):
-    boxes, width = kern.shape[1], block[0].shape[1]
-    return pl.pallas_call(
-        functools.partial(mid_body, len(block)),
-        in_specs=[VMEM] * (3 + len(block)),
-        out_specs=VMEM,
-        out_shape=jax.ShapeDtypeStruct((2, boxes, width), jnp.float32),
-        scratch_shapes=[pltpu.VMEM((2 * boxes, width), jnp.bfloat16)],
+        in_specs=[VMEM] * len(args),
+        out_specs=spec,
+        out_shape=out,
+        scratch_shapes=[pltpu.VMEM((depth, width), jnp.bfloat16)] * len(blocks),
         compiler_params=PARAMS,
         cost_estimate=cost(2),
-    )(kern, *block, low, high)
-
-
-def end_body(kern_ref, x_ref, y_ref, acc_ref, whole_ref, out_ref, p_ref):
-    boxes = p_ref.shape[0] // 2
+    )(*args)
+
+
+def end_body(f, which, kern_ref, x_ref, y_ref, acc_ref, whole_ref, out_ref, p_ref):
     step = pl.program_id(0)
     tile = out_ref.shape[2]
 
@@ -260,21 +263,22 @@
         p_ref[...] = choose((x_ref, y_ref), slice(None))
 
     rows = pl.ds(pl.multiple_of(step * tile, tile), tile)
-    re, im = product(kern_ref[0, rows], kern_ref[1, rows], p_ref[:boxes], p_ref[boxes:])
+    re, im = part(kern_ref, f, p_ref[...], which, rows)
     out_ref[0, 0] = acc_ref[0, rows] + re
     out_ref[0, 1] = acc_ref[1, rows] + im
 
 
-def end(kern, block, acc, out):
-    boxes, width = kern.shape[1], block[0].shape[1]
+def end(f, which, kern, block, acc, out):
+    depth, width = block[0].shape
+    boxes = kern.shape[2]
     tile = boxes // 2
     return pl.pallas_call(
-        end_body,
+        functools.partial(end_body, f, which),
         grid=(2,),
         in_specs=[VMEM] * 4 + [ANY],
-        out_specs=pl.BlockSpec((1, 2, tile, width), lambda i: (1, 0, i, 0)),
+        out_specs=pl.BlockSpec((1, 2, tile, width), lambda i: (f, 0, i, 0)),
         out_shape=jax.ShapeDtypeStruct(out.shape, jnp.float32),
-        scratch_shapes=[pltpu.VMEM((2 * boxes, width), jnp.bfloat16)],
+        scratch_shapes=[pltpu.VMEM((depth, width), jnp.bfloat16)],
         input_output_aliases={4: 0},
         compiler_params=PARAMS,
         cost_estimate=cost(2),
@@ -311,27 +315,38 @@
     send, recv, rows = prepare(
         positions, spans, box_panel, panel_dihedral, freq_table, freq_index
     )
-    first = jnp.concatenate([pressures[0].reshape(2 * boxes, width), rows], axis=0)
-    second = pressures[1].reshape(2 * boxes, width)
-    crossed0 = move(first, cross)
-    crossed1 = move(second, cross)
+    chunks = [
+        jnp.concatenate([pressures[1, 0], rows], axis=0),
+        pressures[0].reshape(2 * boxes, width),
+        pressures[1, 1],
+    ]
+    crossed = [move(c, cross) for c in chunks]
     beside = move(pressures, pair)
     send1 = move(send, pair)
-    terms = functools.partial(near, recv, send, send1, first, second, beside)
-    low = terms(0)
-    high = terms(1)
-    crossed0, crossed1, low, high = lax.optimization_barrier((crossed0, crossed1, low, high))
-    spread0 = move(crossed0, spread)
-    inner0 = move(crossed0, inner)
-    spread1 = move(crossed1, spread)
-    inner1 = move(crossed1, inner)
+    base = near(recv, send, send1, pressures, beside)
+
+    def onward(block):
+        return move(block, spread), move(block, inner)
+
+    first, second, base = lax.optimization_barrier((crossed[0], crossed[1], base))
+    third, base = lax.optimization_barrier((crossed[2], base))
+    spread0, inner0 = onward(first)
+    spread1, inner1 = onward(second)
+    spread2, inner2 = onward(third)
+    spread0 = ordered(spread0, inner1, inner2)
     last0 = move(spread0, last)
-    total0, kern_a = far(recv, (spread0, inner0, crossed0), [low, high], False)
-    out, kern_b = far(recv, (last0, spread0), [total0], True)
-    spread1 = ordered(spread1, out)
+    block0 = (spread0, inner0, first)
+    kern_a = build(recv, block0)
+    kern_b = build(recv, (last0, spread0))
+    total = fold(1, 0, [kern_a, kern_b], [block0, (last0, spread0)], [base])
+    spread1 = ordered(spread1, total)
     last1 = move(spread1, last)
-    total1 = mid(kern_a, (spread1, inner1, crossed1), low, high)
-    return end(kern_b, (last1, spread1), total1, out)
+    part0 = fold(0, 2, [kern_a], [(spread1, inner1, second)], [base])
+    out = fold(0, 2, [kern_b], [(last1, spread1)], [part0], True)
+    spread2 = ordered(spread2, out, total)
+    last2 = move(spread2, last)
+    total = fold(1, 1, [kern_a], [(spread2, inner2, third)], [total])
+    return end(1, 1, kern_b, (last2, spread2), total, out)
 
 
 def solution(mesh):

time: 68.6 us -> 65.6 us (0.956)
  waiting for transfers between devices: 10.5 us -> 2.53 us
  starting transfers between devices: 28.8 us -> 34 us
    ppermute x10 -> x14, waiting for transfers between devices: 10.5 us -> 2.53 us  [move(): return lax.ppermute(block, 'wide', pairs)]
    ppermute x10 -> x14, starting transfers between devices: 28.8 us -> 34 us  [move(): return lax.ppermute(block, 'wide', pairs)]
    pallas_call x6 -> x8, Pallas kernels: 27.1 us -> 26.9 us  [the longest x1 11.8 us: near(): pl.pallas_call(near_body, in_specs=[VMEM] * 5, out_specs=VMEM, out_shape=...]
  transfers between devices with their start and end apart: 10 -> 14, of which waited for: 4 -> 5; matrix products, arithmetic and copies ran while one was open for 0% -> 0% of each run, Pallas kernels for 38% -> 40%
where the time goes in v2:
time: 65.6 us; the launch traced here: 65 us
  starting transfers between devices  34 us (52%)
  Pallas kernels  28 us (43%)
  waiting for transfers between devices  2.53 us (4%)
    ppermute x14, starting transfers between devices, move(): return lax.ppermute(block, 'wide', pairs)  34 us
    pallas_call x1, Pallas kernels, near(): pl.pallas_call(near_body, in_specs=[VMEM] * 5, out_specs=VMEM, out_shape=...  11.8 us
    pallas_call x2, Pallas kernels, build(): pl.pallas_call(functools.partial(build_body, len(block)), in_specs=[VMEM]...  7.26 us
    pallas_call x4, Pallas kernels, fold(): pl.pallas_call(functools.partial(fold_body, f, which, [len(b) for b in bl...  5.89 us
    ppermute x14, waiting for transfers between devices, move(): return lax.ppermute(block, 'wide', pairs)  2.53 us
    pallas_call x1, Pallas kernels, end(): pl.pallas_call(functools.partial(end_body, f, which), grid=(2,), in_specs...  1.92 us
  transfers between devices with their start and end apart: 14, of which 5 were waited for; matrix products, arithmetic and copies ran while one was open for 0% of the time, Pallas kernels for 40%

profile of v2, /device:TPU:1, one launch (start us, length us, event | category | flops | bytes accessed | tf_op | source)
XLA Modules:
  0.0 65.0 jit_solution(7608599828574607187)
XLA Ops:
  0.0 0.1 collective-permute-start.3
  0.1 1.1 %shard_map.73 = (f32[8,512]{1,0:T(8,128)S(1)}, f32[512,8]{1,0:T(8,128)S(1)}, bf16[32,512]{1,0:T(8,128)(2,1)S(1)}) custom-call(f32[3,512]{1,0:T(4,128)} %pos_any.1, f32[512]{0:T(512)} %span_any.1, s32[512]{0:T(512)} %panel_any.1, f32[64]{0:T(128)} %dihedral_any.1, f32[16]{0:T(128)} %table_any.1, s32[2]{0:T(128)} %index_any.1), custom_call_target="tpu_custom_call" | custom-call | flops 17179869184 | bytes 1 | tf_op jit(solution)/shard_map/pallas_call | solution.py:73
  1.2 0.6 collective-permute-start.2
  1.8 0.1 slice_bitcast_fusion
  1.9 0.7 %collective-permute-start = (bf16[544,512]{1,0:T(8,128)(2,1)S(1)}, bf16[544,512]{1,0:T(8,128)(2,1)S(1)}, u32[]{:S(2)}, u32[]{:S(2)}) collective-permute-start(bf16[544,512]{1,0:T(8,128)(2,1)S(1)} %pad_maximum_fusion), channel_id=1, source_target_pairs={{0,2},{2,0},{4,6},{6,4},{8,10},{10,8},{12,14},{14,12},{3,7},{7,11}... | collective-permute-start | bytes 1671176 | tf_op jit(solution)/shard_map/ppermute | solution.py:289
  2.6 0.1 slice.10
  2.7 0.7 %collective-permute-start.1 = (bf16[1024,512]{1,0:T(8,128)(2,1)S(1)}, bf16[1024,512]{1,0:T(8,128)(2,1)S(1)}, u32[]{:S(2)}, u32[]{:S(2)}) collective-permute-start(bf16[1024,512]{1,0:T(8,128)(2,1)S(1)} %bitcast.5), channel_id=1, source_target_pairs={{0,2},{2,0},{4,6},{6,4},{8,10},{10,8},{12,14},{14,12},{3,7},{7,11}... | collective-permute-start | bytes 3145736 | tf_op jit(solution)/shard_map/ppermute | solution.py:289
  3.4 0.7 %collective-permute-start.6 = (bf16[512,512]{1,0:T(8,128)(2,1)S(1)}, bf16[512,512]{1,0:T(8,128)(2,1)S(1)}, u32[]{:S(2)}, u32[]{:S(2)}) collective-permute-start(bf16[512,512]{1,0:T(8,128)(2,1)S(1)} %get-tuple-element.27), channel_id=1, source_target_pairs={{0,2},{2,0},{4,6},{6,4},{8,10},{10,8},{12,14},{14,12},{3,7},{7,11}... | collective-permute-start | bytes 1572872 | tf_op jit(solution)/shard_map/ppermute | solution.py:289
  4.1 0.1 collective-permute-done.2.send1_ref
  4.2 0.2 collective-permute-done.3.p1_ref
  4.4 11.8 %shard_map.74.refs_7_.refs_4_ = f32[2,2,512,512]{3,2,1,0:T(8,128)S(1)} custom-call(f32[512,8]{1,0:T(8,128)S(1)} %get-tuple-element.16.recv_ref, f32[8,512]{1,0:T(8,128)S(1)} %get-tuple-element.18.send0_ref, f32[8,512]{1,0:T(8,128)S(1)} %collective-permute-done.2.send1_ref, bf16[2,2,512,512]{3,2,1,0:T(8,128)(2,1)S(1)} %copy-done, ...), custom_call_target="tpu_custom_call" | custom-call | flops 103079215104 | bytes 1 | tf_op jit(solution)/shard_map/pallas_call | solution.py:163
  16.2 0.0 collective-permute-done.rest_2_.refs_4_
  16.2 0.0 collective-permute-done.1.refs_3_
  16.2 1.3 %collective-permute-start.5 = (bf16[1024,512]{1,0:T(8,128)(2,1)S(1)}, bf16[1024,512]{1,0:T(8,128)(2,1)S(1)}, u32[]{:S(2)}, u32[]{:S(2)}) collective-permute-start(bf16[1024,512]{1,0:T(8,128)(2,1)S(1)} %collective-permute-done.1.refs_3_), channel_id=1, source_target_pairs={{0,1},{4,5},{8,9},{12,13},{16,17},{20,21},{24,25},{28,29}} | collective-permute-start | bytes 3145736 | tf_op jit(solution)/shard_map/ppermute | solution.py:289
  17.5 10.4 %collective-permute-start.4 = (bf16[544,512]{1,0:T(8,128)(2,1)S(1)}, bf16[544,512]{1,0:T(8,128)(2,1)S(1)}, u32[]{:S(2)}, u32[]{:S(2)}) collective-permute-start(bf16[544,512]{1,0:T(8,128)(2,1)S(1)} %collective-permute-done.rest_2_.refs_4_), channel_id=1, source_target_pairs={{1,2},{3,1},{0,4},{6,3},{5,6},{7,5},{4,8},{10,7},{9,10},{11,9},{8,... | collective-permute-start | bytes 1671176 | tf_op jit(solution)/shard_map/ppermute | solution.py:289
  27.9 1.3 %collective-permute-start.11 = (bf16[544,512]{1,0:T(8,128)(2,1)S(1)}, bf16[544,512]{1,0:T(8,128)(2,1)S(1)}, u32[]{:S(2)}, u32[]{:S(2)}) collective-permute-start(bf16[544,512]{1,0:T(8,128)(2,1)S(1)} %collective-permute-done.rest_2_.refs_4_), channel_id=1, source_target_pairs={{0,1},{4,5},{8,9},{12,13},{16,17},{20,21},{24,25},{28,29}} | collective-permute-start | bytes 1671176 | tf_op jit(solution)/shard_map/ppermute | solution.py:289
  29.2 1.3 %collective-permute-start.7 = (bf16[512,512]{1,0:T(8,128)(2,1)S(1)}, bf16[512,512]{1,0:T(8,128)(2,1)S(1)}, u32[]{:S(2)}, u32[]{:S(2)}) collective-permute-start(bf16[512,512]{1,0:T(8,128)(2,1)S(1)} %collective-permute-done.6.refs_3_), channel_id=1, source_target_pairs={{0,1},{4,5},{8,9},{12,13},{16,17},{20,21},{24,25},{28,29}} | collective-permute-start | bytes 1572872 | tf_op jit(solution)/shard_map/ppermute | solution.py:289
  30.5 4.8 %collective-permute-start.10 = (bf16[1024,512]{1,0:T(8,128)(2,1)S(1)}, bf16[1024,512]{1,0:T(8,128)(2,1)S(1)}, u32[]{:S(2)}, u32[]{:S(2)}) collective-permute-start(bf16[1024,512]{1,0:T(8,128)(2,1)S(1)} %collective-permute-done.1.refs_3_), channel_id=1, source_target_pairs={{1,2},{3,1},{0,4},{6,3},{5,6},{7,5},{4,8},{10,7},{9,10},{11,9},{8,... | collective-permute-start | bytes 3145736 | tf_op jit(solution)/shard_map/ppermute | solution.py:289
  35.2 0.7 %collective-permute-start.9 = (bf16[512,512]{1,0:T(8,128)(2,1)S(1)}, bf16[512,512]{1,0:T(8,128)(2,1)S(1)}, u32[]{:S(2)}, u32[]{:S(2)}) collective-permute-start(bf16[512,512]{1,0:T(8,128)(2,1)S(1)} %collective-permute-done.6.refs_3_), channel_id=1, source_target_pairs={{1,2},{3,1},{0,4},{6,3},{5,6},{7,5},{4,8},{10,7},{9,10},{11,9},{8,... | collective-permute-start | bytes 1572872 | tf_op jit(solution)/shard_map/ppermute | solution.py:289
  35.9 0.8 %collective-permute-done.4.rest_1_.rest_0_.refs_2_.refs_6_ = bf16[544,512]{1,0:T(8,128)(2,1)S(1)} collective-permute-done((bf16[544,512]{1,0:T(8,128)(2,1)S(1)}, bf16[544,512]{1,0:T(8,128)(2,1)S(1)}, u32[]{:S(2)}, u32[]{:S(2)}) %collective-permute-start.4) | collective-permute-done | bytes 557088 | tf_op jit(solution)/shard_map/ppermute | solution.py:289
  36.7 4.6 %collective-permute-start.8 = (bf16[544,512]{1,0:T(8,128)(2,1)S(1)}, bf16[544,512]{1,0:T(8,128)(2,1)S(1)}, u32[]{:S(2)}, u32[]{:S(2)}) collective-permute-start(bf16[544,512]{1,0:T(8,128)(2,1)S(1)} %collective-permute-done.4.rest_1_.rest_0_.refs_2_.refs_6_), channel_id=1, source_target_pairs={{1,0},{2,3},{5,4},{6,7},{9,8},{10,11},{13,12},{14,15},{17,16},{18,... | collective-permute-start | bytes 1671176 | tf_op jit(solution)/shard_map/ppermute | solution.py:289
  41.2 3.6 %shard_map.76.refs_0_ = bf16[2,2,512,512]{3,2,1,0:T(8,128)(2,1)S(1)} custom-call(f32[512,8]{1,0:T(8,128)S(1)} %get-tuple-element.16.recv_ref, bf16[544,512]{1,0:T(8,128)(2,1)S(1)} %collective-permute-done.4.rest_1_.rest_0_.refs_2_.refs_6_, bf16[544,512]{1,0:T(8,128)(2,1)S(1)} %collective-permute-done.11.rest_1_.refs_3_, ...), custom_call_target="tpu_custom_call" | custom-call | flops 34359738368 | bytes 1 | tf_op jit(solution)/shard_map/pallas_call | solution.py:192
  44.9 3.6 %shard_map.75.refs_1_.refs_0_.kern_ref = bf16[2,2,512,512]{3,2,1,0:T(8,128)(2,1)S(1)} custom-call(f32[512,8]{1,0:T(8,128)S(1)} %get-tuple-element.16.recv_ref, bf16[544,512]{1,0:T(8,128)(2,1)S(1)} %collective-permute-done.8.rest_0_.refs_5_, bf16[544,512]{1,0:T(8,128)(2,1)S(1)} %collective-permute-done.4.rest_1_.rest_0_.refs_2_.refs_6_), custom_call_target="tpu_custom_call" | custom-call | flops 34359738368 | bytes 1 | tf_op jit(solution)/shard_map/pallas_call | solution.py:192
  48.5 1.3 %shard_map.77.refs_4_ = f32[2,512,512]{2,1,0:T(8,128)S(1)} custom-call(bf16[2,2,512,512]{3,2,1,0:T(8,128)(2,1)S(1)} %shard_map.76.refs_0_, bf16[2,2,512,512]{3,2,1,0:T(8,128)(2,1)S(1)} %shard_map.75.refs_1_.refs_0_.kern_ref, bf16[544,512]{1,0:T(8,128)(2,1)S(1)} %collective-permute-done.4.rest_1_.rest_0_.refs_2_.refs_6_, ...), custom_call_target="tpu_custom_call" | custom-call | flops 17179869184 | bytes 1 | tf_op jit(solution)/shard_map/pallas_call | solution.py:245
  49.8 4.8 %collective-permute-start.12 = (bf16[1024,512]{1,0:T(8,128)(2,1)S(1)}, bf16[1024,512]{1,0:T(8,128)(2,1)S(1)}, u32[]{:S(2)}, u32[]{:S(2)}) collective-permute-start(bf16[1024,512]{1,0:T(8,128)(2,1)S(1)} %collective-permute-done.10.refs_1_.refs_2_), channel_id=1, source_target_pairs={{1,0},{2,3},{5,4},{6,7},{9,8},{10,11},{13,12},{14,15},{17,16},{18,... | collective-permute-start | bytes 3145736 | tf_op jit(solution)/shard_map/ppermute | solution.py:289
  54.6 1.3 %shard_map.78.refs_3_ = f32[2,512,512]{2,1,0:T(8,128)S(1)} custom-call(bf16[2,2,512,512]{3,2,1,0:T(8,128)(2,1)S(1)} %shard_map.76.refs_0_, bf16[1024,512]{1,0:T(8,128)(2,1)S(1)} %collective-permute-done.10.refs_1_.refs_2_, bf16[1024,512]{1,0:T(8,128)(2,1)S(1)} %collective-permute-done.5.refs_2_, bf16[1024,512]{1,0:T(8,128)(2,1)S(1)} %collective-permute-done.1.refs_3_, ...), custom_call_target="tpu_custom_call" | custom-call | flops 17179869184 | bytes 1 | tf_op jit(solution)/shard_map/pallas_call | solution.py:245
  55.9 0.7 %collective-permute-done.12.refs_1_ = bf16[1024,512]{1,0:T(8,128)(2,1)S(1)} collective-permute-done((bf16[1024,512]{1,0:T(8,128)(2,1)S(1)}, bf16[1024,512]{1,0:T(8,128)(2,1)S(1)}, u32[]{:S(2)}, u32[]{:S(2)}) %collective-permute-start.12) | collective-permute-done | bytes 1048608 | tf_op jit(solution)/shard_map/ppermute | solution.py:289
  56.7 2.6 %shard_map.79.whole_ref = f32[2,2,512,512]{3,2,1,0:T(8,128)} custom-call(bf16[2,2,512,512]{3,2,1,0:T(8,128)(2,1)S(1)} %shard_map.75.refs_1_.refs_0_.kern_ref, bf16[1024,512]{1,0:T(8,128)(2,1)S(1)} %collective-permute-done.12.refs_1_, bf16[1024,512]{1,0:T(8,128)(2,1)S(1)} %collective-permute-done.10.refs_1_.refs_2_, f32[2,512,512]{2,1,0:T(8,128)S(1)} %shard_map.78.refs_3_), custom_call_target="tpu_custom_call" | custom-call | flops 17179869184 | bytes 1 | tf_op jit(solution)/shard_map/pallas_call | solution.py:245
  59.3 2.3 %collective-permute-start.13 = (bf16[512,512]{1,0:T(8,128)(2,1)S(1)}, bf16[512,512]{1,0:T(8,128)(2,1)S(1)}, u32[]{:S(2)}, u32[]{:S(2)}) collective-permute-start(bf16[512,512]{1,0:T(8,128)(2,1)S(1)} %collective-permute-done.9.refs_1_.y_ref), channel_id=1, source_target_pairs={{1,0},{2,3},{5,4},{6,7},{9,8},{10,11},{13,12},{14,15},{17,16},{18,... | collective-permute-start | bytes 1572872 | tf_op jit(solution)/shard_map/ppermute | solution.py:289
  61.6 0.7 %shard_map.80.acc_ref = f32[2,512,512]{2,1,0:T(8,128)S(1)} custom-call(bf16[2,2,512,512]{3,2,1,0:T(8,128)(2,1)S(1)} %shard_map.76.refs_0_, bf16[512,512]{1,0:T(8,128)(2,1)S(1)} %collective-permute-done.9.refs_1_.y_ref, bf16[512,512]{1,0:T(8,128)(2,1)S(1)} %collective-permute-done.7.refs_2_, bf16[512,512]{1,0:T(8,128)(2,1)S(1)} %collective-permute-done.6.refs_3_, ...), custom_call_target="tpu_custom_call" | custom-call | flops 17179869184 | bytes 1 | tf_op jit(solution)/shard_map/pallas_call | solution.py:245
  62.3 0.8 %collective-permute-done.13.x_ref = bf16[512,512]{1,0:T(8,128)(2,1)S(1)} collective-permute-done((bf16[512,512]{1,0:T(8,128)(2,1)S(1)}, bf16[512,512]{1,0:T(8,128)(2,1)S(1)}, u32[]{:S(2)}, u32[]{:S(2)}) %collective-permute-start.13) | collective-permute-done | bytes 524320 | tf_op jit(solution)/shard_map/ppermute | solution.py:289
  63.1 1.9 %shard_map.81 = f32[2,2,512,512]{3,2,1,0:T(8,128)} custom-call(bf16[2,2,512,512]{3,2,1,0:T(8,128)(2,1)S(1)} %shard_map.75.refs_1_.refs_0_.kern_ref, bf16[512,512]{1,0:T(8,128)(2,1)S(1)} %collective-permute-done.13.x_ref, bf16[512,512]{1,0:T(8,128)(2,1)S(1)} %collective-permute-done.9.refs_1_.y_ref, ...), custom_call_target="tpu_custom_call", output_to_operand_aliasing={{}: (4, {})} | custom-call | flops 17179869184 | bytes 1 | tf_op jit(solution)/shard_map/pallas_call | solution.py:275
  (10 shorter events, 0.1 us)
Async XLA Ops:
  0.0 1.8 %copy-start = (bf16[2,2,512,512]{3,2,1,0:T(8,128)(2,1)S(1)}, bf16[2,2,512,512]{3,2,1,0:T(8,128)(2,1)}, u32[]{:S(2)}) copy-start(bf16[2,2,512,512]{3,2,1,0:T(8,128)(2,1)} %p0_ref.1) | copy-start | bytes 6291460
  0.0 4.4 %collective-permute-start.3 = (bf16[2,2,512,512]{3,2,1,0:T(8,128)(2,1)}, bf16[2,2,512,512]{3,2,1,0:T(8,128)(2,1)S(1)}, u32[]{:S(2)}, u32[]{:S(2)}) collective-permute-start(bf16[2,2,512,512]{3,2,1,0:T(8,128)(2,1)} %p0_ref.1), channel_id=1, source_target_pairs={{0,1},{1,0},{2,3},{3,2},{4,5},{5,4},{6,7},{7,6},{8,9},{9,8},{10,11... | collective-permute-start | bytes 6291464 | tf_op jit(solution)/shard_map/ppermute | solution.py:289
  1.2 3.0 %collective-permute-start.2 = (f32[8,512]{1,0:T(8,128)S(1)}, f32[8,512]{1,0:T(8,128)S(1)}, u32[]{:S(2)}, u32[]{:S(2)}) collective-permute-start(f32[8,512]{1,0:T(8,128)S(1)} %get-tuple-element.18.send0_ref), channel_id=1, source_target_pairs={{0,1},{1,0},{2,3},{3,2},{4,5},{5,4},{6,7},{7,6},{8,9},{9,8},{10,11... | collective-permute-start | bytes 49160 | tf_op jit(solution)/shard_map/ppermute | solution.py:289
  1.9 14.3 %collective-permute-start = (bf16[544,512]{1,0:T(8,128)(2,1)S(1)}, bf16[544,512]{1,0:T(8,128)(2,1)S(1)}, u32[]{:S(2)}, u32[]{:S(2)}) collective-permute-start(bf16[544,512]{1,0:T(8,128)(2,1)S(1)} %pad_maximum_fusion), channel_id=1, source_target_pairs={{0,2},{2,0},{4,6},{6,4},{8,10},{10,8},{12,14},{14,12},{3,7},{7,11}... | collective-permute-start | bytes 1671176 | tf_op jit(solution)/shard_map/ppermute | solution.py:289
  2.7 13.5 %collective-permute-start.1 = (bf16[1024,512]{1,0:T(8,128)(2,1)S(1)}, bf16[1024,512]{1,0:T(8,128)(2,1)S(1)}, u32[]{:S(2)}, u32[]{:S(2)}) collective-permute-start(bf16[1024,512]{1,0:T(8,128)(2,1)S(1)} %bitcast.5), channel_id=1, source_target_pairs={{0,2},{2,0},{4,6},{6,4},{8,10},{10,8},{12,14},{14,12},{3,7},{7,11}... | collective-permute-start | bytes 3145736 | tf_op jit(solution)/shard_map/ppermute | solution.py:289
  3.4 25.7 %collective-permute-start.6 = (bf16[512,512]{1,0:T(8,128)(2,1)S(1)}, bf16[512,512]{1,0:T(8,128)(2,1)S(1)}, u32[]{:S(2)}, u32[]{:S(2)}) collective-permute-start(bf16[512,512]{1,0:T(8,128)(2,1)S(1)} %get-tuple-element.27), channel_id=1, source_target_pairs={{0,2},{2,0},{4,6},{6,4},{8,10},{10,8},{12,14},{14,12},{3,7},{7,11}... | collective-permute-start | bytes 1572872 | tf_op jit(solution)/shard_map/ppermute | solution.py:289
  16.2 20.4 %collective-permute-start.5 = (bf16[1024,512]{1,0:T(8,128)(2,1)S(1)}, bf16[1024,512]{1,0:T(8,128)(2,1)S(1)}, u32[]{:S(2)}, u32[]{:S(2)}) collective-permute-start(bf16[1024,512]{1,0:T(8,128)(2,1)S(1)} %collective-permute-done.1.refs_3_), channel_id=1, source_target_pairs={{0,1},{4,5},{8,9},{12,13},{16,17},{20,21},{24,25},{28,29}} | collective-permute-start | bytes 3145736 | tf_op jit(solution)/shard_map/ppermute | solution.py:289
  17.5 19.1 %collective-permute-start.4 = (bf16[544,512]{1,0:T(8,128)(2,1)S(1)}, bf16[544,512]{1,0:T(8,128)(2,1)S(1)}, u32[]{:S(2)}, u32[]{:S(2)}) collective-permute-start(bf16[544,512]{1,0:T(8,128)(2,1)S(1)} %collective-permute-done.rest_2_.refs_4_), channel_id=1, source_target_pairs={{1,2},{3,1},{0,4},{6,3},{5,6},{7,5},{4,8},{10,7},{9,10},{11,9},{8,... | collective-permute-start | bytes 1671176 | tf_op jit(solution)/shard_map/ppermute | solution.py:289
  27.9 13.4 %collective-permute-start.11 = (bf16[544,512]{1,0:T(8,128)(2,1)S(1)}, bf16[544,512]{1,0:T(8,128)(2,1)S(1)}, u32[]{:S(2)}, u32[]{:S(2)}) collective-permute-start(bf16[544,512]{1,0:T(8,128)(2,1)S(1)} %collective-permute-done.rest_2_.refs_4_), channel_id=1, source_target_pairs={{0,1},{4,5},{8,9},{12,13},{16,17},{20,21},{24,25},{28,29}} | collective-permute-start | bytes 1671176 | tf_op jit(solution)/shard_map/ppermute | solution.py:289
  29.2 6.1 %collective-permute-start.7 = (bf16[512,512]{1,0:T(8,128)(2,1)S(1)}, bf16[512,512]{1,0:T(8,128)(2,1)S(1)}, u32[]{:S(2)}, u32[]{:S(2)}) collective-permute-start(bf16[512,512]{1,0:T(8,128)(2,1)S(1)} %collective-permute-done.6.refs_3_), channel_id=1, source_target_pairs={{0,1},{4,5},{8,9},{12,13},{16,17},{20,21},{24,25},{28,29}} | collective-permute-start | bytes 1572872 | tf_op jit(solution)/shard_map/ppermute | solution.py:289
  30.5 19.3 %collective-permute-start.10 = (bf16[1024,512]{1,0:T(8,128)(2,1)S(1)}, bf16[1024,512]{1,0:T(8,128)(2,1)S(1)}, u32[]{:S(2)}, u32[]{:S(2)}) collective-permute-start(bf16[1024,512]{1,0:T(8,128)(2,1)S(1)} %collective-permute-done.1.refs_3_), channel_id=1, source_target_pairs={{1,2},{3,1},{0,4},{6,3},{5,6},{7,5},{4,8},{10,7},{9,10},{11,9},{8,... | collective-permute-start | bytes 3145736 | tf_op jit(solution)/shard_map/ppermute | solution.py:289
  35.2 24.0 %collective-permute-start.9 = (bf16[512,512]{1,0:T(8,128)(2,1)S(1)}, bf16[512,512]{1,0:T(8,128)(2,1)S(1)}, u32[]{:S(2)}, u32[]{:S(2)}) collective-permute-start(bf16[512,512]{1,0:T(8,128)(2,1)S(1)} %collective-permute-done.6.refs_3_), channel_id=1, source_target_pairs={{1,2},{3,1},{0,4},{6,3},{5,6},{7,5},{4,8},{10,7},{9,10},{11,9},{8,... | collective-permute-start | bytes 1572872 | tf_op jit(solution)/shard_map/ppermute | solution.py:289
  36.7 8.2 %collective-permute-start.8 = (bf16[544,512]{1,0:T(8,128)(2,1)S(1)}, bf16[544,512]{1,0:T(8,128)(2,1)S(1)}, u32[]{:S(2)}, u32[]{:S(2)}) collective-permute-start(bf16[544,512]{1,0:T(8,128)(2,1)S(1)} %collective-permute-done.4.rest_1_.rest_0_.refs_2_.refs_6_), channel_id=1, source_target_pairs={{1,0},{2,3},{5,4},{6,7},{9,8},{10,11},{13,12},{14,15},{17,16},{18,... | collective-permute-start | bytes 1671176 | tf_op jit(solution)/shard_map/ppermute | solution.py:289
  49.8 6.9 %collective-permute-start.12 = (bf16[1024,512]{1,0:T(8,128)(2,1)S(1)}, bf16[1024,512]{1,0:T(8,128)(2,1)S(1)}, u32[]{:S(2)}, u32[]{:S(2)}) collective-permute-start(bf16[1024,512]{1,0:T(8,128)(2,1)S(1)} %collective-permute-done.10.refs_1_.refs_2_), channel_id=1, source_target_pairs={{1,0},{2,3},{5,4},{6,7},{9,8},{10,11},{13,12},{14,15},{17,16},{18,... | collective-permute-start | bytes 3145736 | tf_op jit(solution)/shard_map/ppermute | solution.py:289
  59.3 3.8 %collective-permute-start.13 = (bf16[512,512]{1,0:T(8,128)(2,1)S(1)}, bf16[512,512]{1,0:T(8,128)(2,1)S(1)}, u32[]{:S(2)}, u32[]{:S(2)}) collective-permute-start(bf16[512,512]{1,0:T(8,128)(2,1)S(1)} %collective-permute-done.9.refs_1_.y_ref), channel_id=1, source_target_pairs={{1,0},{2,3},{5,4},{6,7},{9,8},{10,11},{13,12},{14,15},{17,16},{18,... | collective-permute-start | bytes 1572872 | tf_op jit(solution)/shard_map/ppermute | solution.py:289

commit v3 on v2

--- a/solution.py
+++ b/solution.py
@@ -113,8 +113,8 @@
             rho = dy * dy + dz * dz + e2
             d2 = dx * dx + rho
             inv_d = lax.rsqrt(d2)
-            inv = pl.reciprocal(rho, approx=True)
-            inv = inv * (2.0 - rho * inv)
+            inv = lax.rsqrt(rho)
+            inv = inv * inv
             normal_i = ci * dz - si * dy
             normal_j = ec2 * dz - es2 * dy
             planar = ci * ec + si * es
@@ -210,51 +210,45 @@
     return product(kr, ks, p[:boxes], p[boxes:])
 
 
-def fold_body(f, which, n_blocks, n_acc, *refs):
+def fold_body(f, which, n_blocks, *refs):
     kern_refs, refs = refs[: len(n_blocks)], refs[len(n_blocks) :]
     blocks = []
     for n in n_blocks:
         blocks.append(refs[:n])
         refs = refs[n:]
-    acc_refs, (out_ref, *p_refs) = refs[:n_acc], refs[-1 - len(n_blocks) :]
+    acc_ref, (out_ref, *p_refs) = refs[0], refs[-1 - len(n_blocks) :]
     boxes = kern_refs[0].shape[2]
-    out = out_ref.at[0] if len(out_ref.shape) == 4 else out_ref
     for block, p_ref in zip(blocks, p_refs):
         p_ref[...] = choose(block, slice(0, p_ref.shape[0]))
     half = boxes // 2
     for h in range(2):
         rows = slice(h * half, h * half + half)
-        acc = acc_refs[0].at[f] if len(acc_refs[0].shape) == 4 else acc_refs[0]
+        acc = acc_ref.at[f] if len(acc_ref.shape) == 4 else acc_ref
         re, im = acc[0, rows], acc[1, rows]
         for kern_ref, p_ref in zip(kern_refs, p_refs):
             more_re, more_im = part(kern_ref, f, p_ref[...], which, rows)
             re, im = re + more_re, im + more_im
-        out[0, rows] = re
-        out[1, rows] = im
-
-
-def fold(f, which, kerns, blocks, accs, final=False):
+        out_ref[0, rows] = re
+        out_ref[1, rows] = im
+
+
+def fold(f, which, kerns, blocks, acc):
     boxes, width = kerns[0].shape[2], blocks[0][0].shape[1]
     depth = boxes * (2 if which == 2 else 1)
-    if final:
-        out = jax.ShapeDtypeStruct((2, 2, boxes, width), jnp.float32)
-        spec = pl.BlockSpec((1, 2, boxes, width), lambda i: (f, 0, 0, 0))
-    else:
-        out, spec = jax.ShapeDtypeStruct((2, boxes, width), jnp.float32), VMEM
-    args = [*kerns, *[r for block in blocks for r in block], *accs]
-    return pl.pallas_call(
-        functools.partial(fold_body, f, which, [len(b) for b in blocks], len(accs)),
-        grid=(1,),
+    args = [*kerns, *[r for block in blocks for r in block], acc]
+    return pl.pallas_call(
+        functools.partial(fold_body, f, which, [len(b) for b in blocks]),
         in_specs=[VMEM] * len(args),
-        out_specs=spec,
-        out_shape=out,
+        out_specs=VMEM,
+        out_shape=jax.ShapeDtypeStruct((2, boxes, width), jnp.float32),
         scratch_shapes=[pltpu.VMEM((depth, width), jnp.bfloat16)] * len(blocks),
         compiler_params=PARAMS,
         cost_estimate=cost(2),
     )(*args)
 
 
-def end_body(f, which, kern_ref, x_ref, y_ref, acc_ref, whole_ref, out_ref, p_ref):
+def end_body(f, which, kern_ref, x_ref, y_ref, acc_ref, *rest):
+    out_ref, p_ref = rest[-2:]
     step = pl.program_id(0)
     tile = out_ref.shape[2]
 
@@ -268,21 +262,21 @@
     out_ref[0, 1] = acc_ref[1, rows] + im
 
 
-def end(f, which, kern, block, acc, out):
+def end(f, which, kern, block, acc, *out):
     depth, width = block[0].shape
     boxes = kern.shape[2]
     tile = boxes // 2
     return pl.pallas_call(
         functools.partial(end_body, f, which),
         grid=(2,),
-        in_specs=[VMEM] * 4 + [ANY],
+        in_specs=[VMEM] * 4 + [ANY] * len(out),
         out_specs=pl.BlockSpec((1, 2, tile, width), lambda i: (f, 0, i, 0)),
-        out_shape=jax.ShapeDtypeStruct(out.shape, jnp.float32),
+        out_shape=jax.ShapeDtypeStruct((2, 2, boxes, width), jnp.float32),
         scratch_shapes=[pltpu.VMEM((depth, width), jnp.bfloat16)],
-        input_output_aliases={4: 0},
+        input_output_aliases={4: 0} if out else {},
         compiler_params=PARAMS,
         cost_estimate=cost(2),
-    )(kern, *block, acc, out)
+    )(kern, *block, acc, *out)
 
 
 def move(block, pairs):
@@ -331,22 +325,23 @@
     first, second, base = lax.optimization_barrier((crossed[0], crossed[1], base))
     third, base = lax.optimization_barrier((crossed[2], base))
     spread0, inner0 = onward(first)
-    spread1, inner1 = onward(second)
+    spread1 = move(second, spread)
     spread2, inner2 = onward(third)
+    inner1 = move(second, inner)
     spread0 = ordered(spread0, inner1, inner2)
     last0 = move(spread0, last)
     block0 = (spread0, inner0, first)
     kern_a = build(recv, block0)
     kern_b = build(recv, (last0, spread0))
-    total = fold(1, 0, [kern_a, kern_b], [block0, (last0, spread0)], [base])
-    spread1 = ordered(spread1, total)
+    total = fold(1, 0, [kern_a, kern_b], [block0, (last0, spread0)], base)
+    spread2 = ordered(spread2, total)
+    last2 = move(spread2, last)
+    total = fold(1, 1, [kern_a], [(spread2, inner2, third)], total)
+    out = end(1, 1, kern_b, (last2, spread2), total)
+    spread1 = ordered(spread1, out)
     last1 = move(spread1, last)
-    part0 = fold(0, 2, [kern_a], [(spread1, inner1, second)], [base])
-    out = fold(0, 2, [kern_b], [(last1, spread1)], [part0], True)
-    spread2 = ordered(spread2, out, total)
-    last2 = move(spread2, last)
-    total = fold(1, 1, [kern_a], [(spread2, inner2, third)], [total])
-    return end(1, 1, kern_b, (last2, spread2), total, out)
+    part0 = fold(0, 2, [kern_a], [(spread1, inner1, second)], base)
+    return end(0, 2, kern_b, (last1, spread1), part0, out)
 
 
 def solution(mesh):

time: 65.6 us -> 65.4 us (level)
    pallas_call x4 -> x3, Pallas kernels: 5.89 us -> 3.29 us  [fold(): pl.pallas_call(functools.partial(fold_body, f, which, [len(b) for b in bl...]
    pallas_call x1 -> x2, Pallas kernels: 1.92 us -> 4.45 us  [end(): pl.pallas_call(functools.partial(end_body, f, which), grid=(2,), in_specs...]
  transfers between devices with their start and end apart: 14 -> 14, of which waited for: 5 -> 5; matrix products, arithmetic and copies ran while one was open for 0% -> 0% of each run, Pallas kernels for 40% -> 39%
where the time goes in v3:
time: 65.4 us; the launch traced here: 64.8 us
  starting transfers between devices  34 us (52%)
  Pallas kernels  27.7 us (42%)
  waiting for transfers between devices  2.72 us (4%)
    ppermute x14, starting transfers between devices, move(): return lax.ppermute(block, 'wide', pairs)  34 us
    pallas_call x1, Pallas kernels, near(): pl.pallas_call(near_body, in_specs=[VMEM] * 5, out_specs=VMEM, out_shape=...  11.7 us
    pallas_call x2, Pallas kernels, build(): pl.pallas_call(functools.partial(build_body, len(block)), in_specs=[VMEM]...  7.15 us
    pallas_call x2, Pallas kernels, end(): pl.pallas_call(functools.partial(end_body, f, which), grid=(2,), in_specs...  4.45 us
    pallas_call x3, Pallas kernels, fold(): pl.pallas_call(functools.partial(fold_body, f, which, [len(b) for b in bl...  3.29 us
    ppermute x14, waiting for transfers between devices, move(): return lax.ppermute(block, 'wide', pairs)  2.72 us
  transfers between devices with their start and end apart: 14, of which 5 were waited for; matrix products, arithmetic and copies ran while one was open for 0% of the time, Pallas kernels for 39%

profile of v3, /device:TPU:1, one launch (start us, length us, event | category | flops | bytes accessed | tf_op | source)
XLA Modules:
  0.0 64.8 jit_solution(2260298906161951611)
XLA Ops:
  0.0 0.1 collective-permute-start.3
  0.1 1.1 %shard_map.73 = (f32[8,512]{1,0:T(8,128)S(1)}, f32[512,8]{1,0:T(8,128)S(1)}, bf16[32,512]{1,0:T(8,128)(2,1)S(1)}) custom-call(f32[3,512]{1,0:T(4,128)} %pos_any.1, f32[512]{0:T(512)} %span_any.1, s32[512]{0:T(512)} %panel_any.1, f32[64]{0:T(128)} %dihedral_any.1, f32[16]{0:T(128)} %table_any.1, s32[2]{0:T(128)} %index_any.1), custom_call_target="tpu_custom_call" | custom-call | flops 17179869184 | bytes 1 | tf_op jit(solution)/shard_map/pallas_call | solution.py:73
  1.2 0.6 collective-permute-start.2
  1.8 0.1 slice_bitcast_fusion
  1.9 0.7 %collective-permute-start = (bf16[544,512]{1,0:T(8,128)(2,1)S(1)}, bf16[544,512]{1,0:T(8,128)(2,1)S(1)}, u32[]{:S(2)}, u32[]{:S(2)}) collective-permute-start(bf16[544,512]{1,0:T(8,128)(2,1)S(1)} %pad_maximum_fusion), channel_id=1, source_target_pairs={{0,2},{2,0},{4,6},{6,4},{8,10},{10,8},{12,14},{14,12},{3,7},{7,11}... | collective-permute-start | bytes 1671176 | tf_op jit(solution)/shard_map/ppermute | solution.py:283
  2.6 0.1 slice.10
  2.7 0.7 %collective-permute-start.1 = (bf16[1024,512]{1,0:T(8,128)(2,1)S(1)}, bf16[1024,512]{1,0:T(8,128)(2,1)S(1)}, u32[]{:S(2)}, u32[]{:S(2)}) collective-permute-start(bf16[1024,512]{1,0:T(8,128)(2,1)S(1)} %bitcast.5), channel_id=1, source_target_pairs={{0,2},{2,0},{4,6},{6,4},{8,10},{10,8},{12,14},{14,12},{3,7},{7,11}... | collective-permute-start | bytes 3145736 | tf_op jit(solution)/shard_map/ppermute | solution.py:283
  3.4 0.7 %collective-permute-start.6 = (bf16[512,512]{1,0:T(8,128)(2,1)S(1)}, bf16[512,512]{1,0:T(8,128)(2,1)S(1)}, u32[]{:S(2)}, u32[]{:S(2)}) collective-permute-start(bf16[512,512]{1,0:T(8,128)(2,1)S(1)} %get-tuple-element.27), channel_id=1, source_target_pairs={{0,2},{2,0},{4,6},{6,4},{8,10},{10,8},{12,14},{14,12},{3,7},{7,11}... | collective-permute-start | bytes 1572872 | tf_op jit(solution)/shard_map/ppermute | solution.py:283
  4.1 0.1 collective-permute-done.2.send1_ref
  4.2 0.2 collective-permute-done.3.p1_ref
  4.4 11.7 %shard_map.74.refs_7_.refs_4_ = f32[2,2,512,512]{3,2,1,0:T(8,128)S(1)} custom-call(f32[512,8]{1,0:T(8,128)S(1)} %get-tuple-element.16.recv_ref, f32[8,512]{1,0:T(8,128)S(1)} %get-tuple-element.18.send0_ref, f32[8,512]{1,0:T(8,128)S(1)} %collective-permute-done.2.send1_ref, bf16[2,2,512,512]{3,2,1,0:T(8,128)(2,1)S(1)} %copy-done, ...), custom_call_target="tpu_custom_call" | custom-call | flops 103079215104 | bytes 1 | tf_op jit(solution)/shard_map/pallas_call | solution.py:163
  16.1 0.0 collective-permute-done.rest_2_.refs_4_
  16.1 1.3 %collective-permute-start.5 = (bf16[1024,512]{1,0:T(8,128)(2,1)S(1)}, bf16[1024,512]{1,0:T(8,128)(2,1)S(1)}, u32[]{:S(2)}, u32[]{:S(2)}) collective-permute-start(bf16[1024,512]{1,0:T(8,128)(2,1)S(1)} %collective-permute-done.1.refs_3_), channel_id=1, source_target_pairs={{0,1},{4,5},{8,9},{12,13},{16,17},{20,21},{24,25},{28,29}} | collective-permute-start | bytes 3145736 | tf_op jit(solution)/shard_map/ppermute | solution.py:283
  17.4 10.5 %collective-permute-start.4 = (bf16[544,512]{1,0:T(8,128)(2,1)S(1)}, bf16[544,512]{1,0:T(8,128)(2,1)S(1)}, u32[]{:S(2)}, u32[]{:S(2)}) collective-permute-start(bf16[544,512]{1,0:T(8,128)(2,1)S(1)} %collective-permute-done.rest_2_.refs_4_), channel_id=1, source_target_pairs={{1,2},{3,1},{0,4},{6,3},{5,6},{7,5},{4,8},{10,7},{9,10},{11,9},{8,... | collective-permute-start | bytes 1671176 | tf_op jit(solution)/shard_map/ppermute | solution.py:283
  27.9 1.3 %collective-permute-start.11 = (bf16[544,512]{1,0:T(8,128)(2,1)S(1)}, bf16[544,512]{1,0:T(8,128)(2,1)S(1)}, u32[]{:S(2)}, u32[]{:S(2)}) collective-permute-start(bf16[544,512]{1,0:T(8,128)(2,1)S(1)} %collective-permute-done.rest_2_.refs_4_), channel_id=1, source_target_pairs={{0,1},{4,5},{8,9},{12,13},{16,17},{20,21},{24,25},{28,29}} | collective-permute-start | bytes 1671176 | tf_op jit(solution)/shard_map/ppermute | solution.py:283
  29.2 0.0 collective-permute-done.6.refs_3_
  29.2 1.3 %collective-permute-start.7 = (bf16[512,512]{1,0:T(8,128)(2,1)S(1)}, bf16[512,512]{1,0:T(8,128)(2,1)S(1)}, u32[]{:S(2)}, u32[]{:S(2)}) collective-permute-start(bf16[512,512]{1,0:T(8,128)(2,1)S(1)} %collective-permute-done.6.refs_3_), channel_id=1, source_target_pairs={{0,1},{4,5},{8,9},{12,13},{16,17},{20,21},{24,25},{28,29}} | collective-permute-start | bytes 1572872 | tf_op jit(solution)/shard_map/ppermute | solution.py:283
  30.5 4.8 %collective-permute-start.10 = (bf16[512,512]{1,0:T(8,128)(2,1)S(1)}, bf16[512,512]{1,0:T(8,128)(2,1)S(1)}, u32[]{:S(2)}, u32[]{:S(2)}) collective-permute-start(bf16[512,512]{1,0:T(8,128)(2,1)S(1)} %collective-permute-done.6.refs_3_), channel_id=1, source_target_pairs={{1,2},{3,1},{0,4},{6,3},{5,6},{7,5},{4,8},{10,7},{9,10},{11,9},{8,... | collective-permute-start | bytes 1572872 | tf_op jit(solution)/shard_map/ppermute | solution.py:283
  35.2 0.7 %collective-permute-start.9 = (bf16[1024,512]{1,0:T(8,128)(2,1)S(1)}, bf16[1024,512]{1,0:T(8,128)(2,1)S(1)}, u32[]{:S(2)}, u32[]{:S(2)}) collective-permute-start(bf16[1024,512]{1,0:T(8,128)(2,1)S(1)} %collective-permute-done.1.refs_3_), channel_id=1, source_target_pairs={{1,2},{3,1},{0,4},{6,3},{5,6},{7,5},{4,8},{10,7},{9,10},{11,9},{8,... | collective-permute-start | bytes 3145736 | tf_op jit(solution)/shard_map/ppermute | solution.py:283
  35.9 0.8 %collective-permute-done.4.rest_1_.rest_0_.refs_2_.refs_6_ = bf16[544,512]{1,0:T(8,128)(2,1)S(1)} collective-permute-done((bf16[544,512]{1,0:T(8,128)(2,1)S(1)}, bf16[544,512]{1,0:T(8,128)(2,1)S(1)}, u32[]{:S(2)}, u32[]{:S(2)}) %collective-permute-start.4) | collective-permute-done | bytes 557088 | tf_op jit(solution)/shard_map/ppermute | solution.py:283
  36.7 4.6 %collective-permute-start.8 = (bf16[544,512]{1,0:T(8,128)(2,1)S(1)}, bf16[544,512]{1,0:T(8,128)(2,1)S(1)}, u32[]{:S(2)}, u32[]{:S(2)}) collective-permute-start(bf16[544,512]{1,0:T(8,128)(2,1)S(1)} %collective-permute-done.4.rest_1_.rest_0_.refs_2_.refs_6_), channel_id=1, source_target_pairs={{1,0},{2,3},{5,4},{6,7},{9,8},{10,11},{13,12},{14,15},{17,16},{18,... | collective-permute-start | bytes 1671176 | tf_op jit(solution)/shard_map/ppermute | solution.py:283
  41.2 3.6 %shard_map.76.refs_0_ = bf16[2,2,512,512]{3,2,1,0:T(8,128)(2,1)S(1)} custom-call(f32[512,8]{1,0:T(8,128)S(1)} %get-tuple-element.16.recv_ref, bf16[544,512]{1,0:T(8,128)(2,1)S(1)} %collective-permute-done.4.rest_1_.rest_0_.refs_2_.refs_6_, bf16[544,512]{1,0:T(8,128)(2,1)S(1)} %collective-permute-done.11.rest_1_.refs_3_, ...), custom_call_target="tpu_custom_call" | custom-call | flops 34359738368 | bytes 1 | tf_op jit(solution)/shard_map/pallas_call | solution.py:192
  44.8 3.6 %shard_map.75.refs_1_.kern_ref = bf16[2,2,512,512]{3,2,1,0:T(8,128)(2,1)S(1)} custom-call(f32[512,8]{1,0:T(8,128)S(1)} %get-tuple-element.16.recv_ref, bf16[544,512]{1,0:T(8,128)(2,1)S(1)} %collective-permute-done.8.rest_0_.refs_5_, bf16[544,512]{1,0:T(8,128)(2,1)S(1)} %collective-permute-done.4.rest_1_.rest_0_.refs_2_.refs_6_), custom_call_target="tpu_custom_call" | custom-call | flops 34359738368 | bytes 1 | tf_op jit(solution)/shard_map/pallas_call | solution.py:192
  48.4 1.3 %shard_map.77.refs_4_ = f32[2,512,512]{2,1,0:T(8,128)S(1)} custom-call(bf16[2,2,512,512]{3,2,1,0:T(8,128)(2,1)S(1)} %shard_map.76.refs_0_, bf16[2,2,512,512]{3,2,1,0:T(8,128)(2,1)S(1)} %shard_map.75.refs_1_.kern_ref, bf16[544,512]{1,0:T(8,128)(2,1)S(1)} %collective-permute-done.4.rest_1_.rest_0_.refs_2_.refs_6_, ...), custom_call_target="tpu_custom_call" | custom-call | flops 17179869184 | bytes 1 | tf_op jit(solution)/shard_map/pallas_call | solution.py:239
  49.7 1.3 %collective-permute-start.12 = (bf16[512,512]{1,0:T(8,128)(2,1)S(1)}, bf16[512,512]{1,0:T(8,128)(2,1)S(1)}, u32[]{:S(2)}, u32[]{:S(2)}) collective-permute-start(bf16[512,512]{1,0:T(8,128)(2,1)S(1)} %collective-permute-done.10.refs_1_.y_ref), channel_id=1, source_target_pairs={{1,0},{2,3},{5,4},{6,7},{9,8},{10,11},{13,12},{14,15},{17,16},{18,... | collective-permute-start | bytes 1572872 | tf_op jit(solution)/shard_map/ppermute | solution.py:283
  51.0 0.7 %shard_map.78.acc_ref = f32[2,512,512]{2,1,0:T(8,128)S(1)} custom-call(bf16[2,2,512,512]{3,2,1,0:T(8,128)(2,1)S(1)} %shard_map.76.refs_0_, bf16[512,512]{1,0:T(8,128)(2,1)S(1)} %collective-permute-done.10.refs_1_.y_ref, bf16[512,512]{1,0:T(8,128)(2,1)S(1)} %collective-permute-done.7.refs_2_, bf16[512,512]{1,0:T(8,128)(2,1)S(1)} %collective-permute-done.6.refs_3_, ...), custom_call_target="tpu_custom_call" | custom-call | flops 17179869184 | bytes 1 | tf_op jit(solution)/shard_map/pallas_call | solution.py:239
  51.8 0.8 %collective-permute-done.12.x_ref = bf16[512,512]{1,0:T(8,128)(2,1)S(1)} collective-permute-done((bf16[512,512]{1,0:T(8,128)(2,1)S(1)}, bf16[512,512]{1,0:T(8,128)(2,1)S(1)}, u32[]{:S(2)}, u32[]{:S(2)}) %collective-permute-start.12) | collective-permute-done | bytes 524320 | tf_op jit(solution)/shard_map/ppermute | solution.py:283
  52.5 1.9 %shard_map.79.rest_0_ = f32[2,2,512,512]{3,2,1,0:T(8,128)} custom-call(bf16[2,2,512,512]{3,2,1,0:T(8,128)(2,1)S(1)} %shard_map.75.refs_1_.kern_ref, bf16[512,512]{1,0:T(8,128)(2,1)S(1)} %collective-permute-done.12.x_ref, bf16[512,512]{1,0:T(8,128)(2,1)S(1)} %collective-permute-done.10.refs_1_.y_ref, f32[2,512,512]{2,1,0:T(8,128)S(1)} %shard_map.78.acc_ref), custom_call_target="tpu_custom_call" | custom-call | flops 17179869184 | bytes 1 | tf_op jit(solution)/shard_map/pallas_call | solution.py:269
  54.5 5.6 %collective-permute-start.13 = (bf16[1024,512]{1,0:T(8,128)(2,1)S(1)}, bf16[1024,512]{1,0:T(8,128)(2,1)S(1)}, u32[]{:S(2)}, u32[]{:S(2)}) collective-permute-start(bf16[1024,512]{1,0:T(8,128)(2,1)S(1)} %collective-permute-done.9.refs_1_.y_ref), channel_id=1, source_target_pairs={{1,0},{2,3},{5,4},{6,7},{9,8},{10,11},{13,12},{14,15},{17,16},{18,... | collective-permute-start | bytes 3145736 | tf_op jit(solution)/shard_map/ppermute | solution.py:283
  60.1 1.3 %shard_map.80.acc_ref = f32[2,512,512]{2,1,0:T(8,128)S(1)} custom-call(bf16[2,2,512,512]{3,2,1,0:T(8,128)(2,1)S(1)} %shard_map.76.refs_0_, bf16[1024,512]{1,0:T(8,128)(2,1)S(1)} %collective-permute-done.9.refs_1_.y_ref, bf16[1024,512]{1,0:T(8,128)(2,1)S(1)} %collective-permute-done.5.refs_2_, bf16[1024,512]{1,0:T(8,128)(2,1)S(1)} %collective-permute-done.1.refs_3_, ...), custom_call_target="tpu_custom_call" | custom-call | flops 17179869184 | bytes 1 | tf_op jit(solution)/shard_map/pallas_call | solution.py:239
  61.4 0.9 %collective-permute-done.13.x_ref = bf16[1024,512]{1,0:T(8,128)(2,1)S(1)} collective-permute-done((bf16[1024,512]{1,0:T(8,128)(2,1)S(1)}, bf16[1024,512]{1,0:T(8,128)(2,1)S(1)}, u32[]{:S(2)}, u32[]{:S(2)}) %collective-permute-start.13) | collective-permute-done | bytes 1048608 | tf_op jit(solution)/shard_map/ppermute | solution.py:283
  62.3 2.5 %shard_map.81 = f32[2,2,512,512]{3,2,1,0:T(8,128)} custom-call(bf16[2,2,512,512]{3,2,1,0:T(8,128)(2,1)S(1)} %shard_map.75.refs_1_.kern_ref, bf16[1024,512]{1,0:T(8,128)(2,1)S(1)} %collective-permute-done.13.x_ref, bf16[1024,512]{1,0:T(8,128)(2,1)S(1)} %collective-permute-done.9.refs_1_.y_ref, ...), custom_call_target="tpu_custom_call", output_to_operand_aliasing={{}: (4, {})} | custom-call | flops 17179869184 | bytes 1 | tf_op jit(solution)/shard_map/pallas_call | solution.py:269
  (10 shorter events, 0.1 us)
Async XLA Ops:
  0.0 1.8 %copy-start = (bf16[2,2,512,512]{3,2,1,0:T(8,128)(2,1)S(1)}, bf16[2,2,512,512]{3,2,1,0:T(8,128)(2,1)}, u32[]{:S(2)}) copy-start(bf16[2,2,512,512]{3,2,1,0:T(8,128)(2,1)} %p0_ref.1) | copy-start | bytes 6291460
  0.0 4.4 %collective-permute-start.3 = (bf16[2,2,512,512]{3,2,1,0:T(8,128)(2,1)}, bf16[2,2,512,512]{3,2,1,0:T(8,128)(2,1)S(1)}, u32[]{:S(2)}, u32[]{:S(2)}) collective-permute-start(bf16[2,2,512,512]{3,2,1,0:T(8,128)(2,1)} %p0_ref.1), channel_id=1, source_target_pairs={{0,1},{1,0},{2,3},{3,2},{4,5},{5,4},{6,7},{7,6},{8,9},{9,8},{10,11... | collective-permute-start | bytes 6291464 | tf_op jit(solution)/shard_map/ppermute | solution.py:283
  1.2 3.0 %collective-permute-start.2 = (f32[8,512]{1,0:T(8,128)S(1)}, f32[8,512]{1,0:T(8,128)S(1)}, u32[]{:S(2)}, u32[]{:S(2)}) collective-permute-start(f32[8,512]{1,0:T(8,128)S(1)} %get-tuple-element.18.send0_ref), channel_id=1, source_target_pairs={{0,1},{1,0},{2,3},{3,2},{4,5},{5,4},{6,7},{7,6},{8,9},{9,8},{10,11... | collective-permute-start | bytes 49160 | tf_op jit(solution)/shard_map/ppermute | solution.py:283
  1.9 14.2 %collective-permute-start = (bf16[544,512]{1,0:T(8,128)(2,1)S(1)}, bf16[544,512]{1,0:T(8,128)(2,1)S(1)}, u32[]{:S(2)}, u32[]{:S(2)}) collective-permute-start(bf16[544,512]{1,0:T(8,128)(2,1)S(1)} %pad_maximum_fusion), channel_id=1, source_target_pairs={{0,2},{2,0},{4,6},{6,4},{8,10},{10,8},{12,14},{14,12},{3,7},{7,11}... | collective-permute-start | bytes 1671176 | tf_op jit(solution)/shard_map/ppermute | solution.py:283
  2.7 13.4 %collective-permute-start.1 = (bf16[1024,512]{1,0:T(8,128)(2,1)S(1)}, bf16[1024,512]{1,0:T(8,128)(2,1)S(1)}, u32[]{:S(2)}, u32[]{:S(2)}) collective-permute-start(bf16[1024,512]{1,0:T(8,128)(2,1)S(1)} %bitcast.5), channel_id=1, source_target_pairs={{0,2},{2,0},{4,6},{6,4},{8,10},{10,8},{12,14},{14,12},{3,7},{7,11}... | collective-permute-start | bytes 3145736 | tf_op jit(solution)/shard_map/ppermute | solution.py:283
  3.4 25.7 %collective-permute-start.6 = (bf16[512,512]{1,0:T(8,128)(2,1)S(1)}, bf16[512,512]{1,0:T(8,128)(2,1)S(1)}, u32[]{:S(2)}, u32[]{:S(2)}) collective-permute-start(bf16[512,512]{1,0:T(8,128)(2,1)S(1)} %get-tuple-element.27), channel_id=1, source_target_pairs={{0,2},{2,0},{4,6},{6,4},{8,10},{10,8},{12,14},{14,12},{3,7},{7,11}... | collective-permute-start | bytes 1572872 | tf_op jit(solution)/shard_map/ppermute | solution.py:283
  16.1 20.6 %collective-permute-start.5 = (bf16[1024,512]{1,0:T(8,128)(2,1)S(1)}, bf16[1024,512]{1,0:T(8,128)(2,1)S(1)}, u32[]{:S(2)}, u32[]{:S(2)}) collective-permute-start(bf16[1024,512]{1,0:T(8,128)(2,1)S(1)} %collective-permute-done.1.refs_3_), channel_id=1, source_target_pairs={{0,1},{4,5},{8,9},{12,13},{16,17},{20,21},{24,25},{28,29}} | collective-permute-start | bytes 3145736 | tf_op jit(solution)/shard_map/ppermute | solution.py:283
  17.4 19.3 %collective-permute-start.4 = (bf16[544,512]{1,0:T(8,128)(2,1)S(1)}, bf16[544,512]{1,0:T(8,128)(2,1)S(1)}, u32[]{:S(2)}, u32[]{:S(2)}) collective-permute-start(bf16[544,512]{1,0:T(8,128)(2,1)S(1)} %collective-permute-done.rest_2_.refs_4_), channel_id=1, source_target_pairs={{1,2},{3,1},{0,4},{6,3},{5,6},{7,5},{4,8},{10,7},{9,10},{11,9},{8,... | collective-permute-start | bytes 1671176 | tf_op jit(solution)/shard_map/ppermute | solution.py:283
  27.9 13.4 %collective-permute-start.11 = (bf16[544,512]{1,0:T(8,128)(2,1)S(1)}, bf16[544,512]{1,0:T(8,128)(2,1)S(1)}, u32[]{:S(2)}, u32[]{:S(2)}) collective-permute-start(bf16[544,512]{1,0:T(8,128)(2,1)S(1)} %collective-permute-done.rest_2_.refs_4_), channel_id=1, source_target_pairs={{0,1},{4,5},{8,9},{12,13},{16,17},{20,21},{24,25},{28,29}} | collective-permute-start | bytes 1671176 | tf_op jit(solution)/shard_map/ppermute | solution.py:283
  29.2 6.1 %collective-permute-start.7 = (bf16[512,512]{1,0:T(8,128)(2,1)S(1)}, bf16[512,512]{1,0:T(8,128)(2,1)S(1)}, u32[]{:S(2)}, u32[]{:S(2)}) collective-permute-start(bf16[512,512]{1,0:T(8,128)(2,1)S(1)} %collective-permute-done.6.refs_3_), channel_id=1, source_target_pairs={{0,1},{4,5},{8,9},{12,13},{16,17},{20,21},{24,25},{28,29}} | collective-permute-start | bytes 1572872 | tf_op jit(solution)/shard_map/ppermute | solution.py:283
  30.5 19.2 %collective-permute-start.10 = (bf16[512,512]{1,0:T(8,128)(2,1)S(1)}, bf16[512,512]{1,0:T(8,128)(2,1)S(1)}, u32[]{:S(2)}, u32[]{:S(2)}) collective-permute-start(bf16[512,512]{1,0:T(8,128)(2,1)S(1)} %collective-permute-done.6.refs_3_), channel_id=1, source_target_pairs={{1,2},{3,1},{0,4},{6,3},{5,6},{7,5},{4,8},{10,7},{9,10},{11,9},{8,... | collective-permute-start | bytes 1572872 | tf_op jit(solution)/shard_map/ppermute | solution.py:283
  35.2 19.2 %collective-permute-start.9 = (bf16[1024,512]{1,0:T(8,128)(2,1)S(1)}, bf16[1024,512]{1,0:T(8,128)(2,1)S(1)}, u32[]{:S(2)}, u32[]{:S(2)}) collective-permute-start(bf16[1024,512]{1,0:T(8,128)(2,1)S(1)} %collective-permute-done.1.refs_3_), channel_id=1, source_target_pairs={{1,2},{3,1},{0,4},{6,3},{5,6},{7,5},{4,8},{10,7},{9,10},{11,9},{8,... | collective-permute-start | bytes 3145736 | tf_op jit(solution)/shard_map/ppermute | solution.py:283
  36.7 8.2 %collective-permute-start.8 = (bf16[544,512]{1,0:T(8,128)(2,1)S(1)}, bf16[544,512]{1,0:T(8,128)(2,1)S(1)}, u32[]{:S(2)}, u32[]{:S(2)}) collective-permute-start(bf16[544,512]{1,0:T(8,128)(2,1)S(1)} %collective-permute-done.4.rest_1_.rest_0_.refs_2_.refs_6_), channel_id=1, source_target_pairs={{1,0},{2,3},{5,4},{6,7},{9,8},{10,11},{13,12},{14,15},{17,16},{18,... | collective-permute-start | bytes 1671176 | tf_op jit(solution)/shard_map/ppermute | solution.py:283
  49.7 2.8 %collective-permute-start.12 = (bf16[512,512]{1,0:T(8,128)(2,1)S(1)}, bf16[512,512]{1,0:T(8,128)(2,1)S(1)}, u32[]{:S(2)}, u32[]{:S(2)}) collective-permute-start(bf16[512,512]{1,0:T(8,128)(2,1)S(1)} %collective-permute-done.10.refs_1_.y_ref), channel_id=1, source_target_pairs={{1,0},{2,3},{5,4},{6,7},{9,8},{10,11},{13,12},{14,15},{17,16},{18,... | collective-permute-start | bytes 1572872 | tf_op jit(solution)/shard_map/ppermute | solution.py:283
  54.5 7.8 %collective-permute-start.13 = (bf16[1024,512]{1,0:T(8,128)(2,1)S(1)}, bf16[1024,512]{1,0:T(8,128)(2,1)S(1)}, u32[]{:S(2)}, u32[]{:S(2)}) collective-permute-start(bf16[1024,512]{1,0:T(8,128)(2,1)S(1)} %collective-permute-done.9.refs_1_.y_ref), channel_id=1, source_target_pairs={{1,0},{2,3},{5,4},{6,7},{9,8},{10,11},{13,12},{14,15},{17,16},{18,... | collective-permute-start | bytes 3145736 | tf_op jit(solution)/shard_map/ppermute | solution.py:283

commit v4 on v2

--- a/solution.py
+++ b/solution.py
@@ -113,8 +113,8 @@
             rho = dy * dy + dz * dz + e2
             d2 = dx * dx + rho
             inv_d = lax.rsqrt(d2)
-            inv = pl.reciprocal(rho, approx=True)
-            inv = inv * (2.0 - rho * inv)
+            inv = lax.rsqrt(rho)
+            inv = inv * inv
             normal_i = ci * dz - si * dy
             normal_j = ec2 * dz - es2 * dy
             planar = ci * ec + si * es
@@ -128,7 +128,7 @@
                 im[at, lanes] = (amp * u * horner(v, SIN_COEF)).astype(jnp.bfloat16)
         return carry
 
-    lax.fori_loop(0, rows // ROWS, row_block, 0, unroll=4)
+    lax.fori_loop(0, rows // ROWS, row_block, 0, unroll=8)
 
 
 def dot(a, b):

time: 65.6 us -> 65.6 us (level)
  Pallas kernels: 28 us -> 27.2 us
  transfers between devices with their start and end apart: 14 -> 14, of which waited for: 5 -> 5; matrix products, arithmetic and copies ran while one was open for 0% -> 0% of each run, Pallas kernels for 40% -> 39%
where the time goes in v4:
time: 65.6 us; the launch traced here: 65 us
  starting transfers between devices  34.6 us (53%)
  Pallas kernels  27.2 us (41%)
  waiting for transfers between devices  2.71 us (4%)
    ppermute x14, starting transfers between devices, move(): return lax.ppermute(block, 'wide', pairs)  34.6 us
    pallas_call x1, Pallas kernels, near(): pl.pallas_call(near_body, in_specs=[VMEM] * 5, out_specs=VMEM, out_shape=...  11.4 us
    pallas_call x2, Pallas kernels, build(): pl.pallas_call(functools.partial(build_body, len(block)), in_specs=[VMEM]...  6.88 us
    pallas_call x4, Pallas kernels, fold(): pl.pallas_call(functools.partial(fold_body, f, which, [len(b) for b in bl...  5.89 us
    ppermute x14, waiting for transfers between devices, move(): return lax.ppermute(block, 'wide', pairs)  2.71 us
    pallas_call x1, Pallas kernels, end(): pl.pallas_call(functools.partial(end_body, f, which), grid=(2,), in_specs...  1.92 us
  transfers between devices with their start and end apart: 14, of which 5 were waited for; matrix products, arithmetic and copies ran while one was open for 0% of the time, Pallas kernels for 39%

profile of v4, /device:TPU:1, one launch (start us, length us, event | category | flops | bytes accessed | tf_op | source)
XLA Modules:
  0.0 65.0 jit_solution(4583037945191424701)
XLA Ops:
  0.0 0.1 collective-permute-start.3
  0.1 1.1 %shard_map.73 = (f32[8,512]{1,0:T(8,128)S(1)}, f32[512,8]{1,0:T(8,128)S(1)}, bf16[32,512]{1,0:T(8,128)(2,1)S(1)}) custom-call(f32[3,512]{1,0:T(4,128)} %pos_any.1, f32[512]{0:T(512)} %span_any.1, s32[512]{0:T(512)} %panel_any.1, f32[64]{0:T(128)} %dihedral_any.1, f32[16]{0:T(128)} %table_any.1, s32[2]{0:T(128)} %index_any.1), custom_call_target="tpu_custom_call" | custom-call | flops 17179869184 | bytes 1 | tf_op jit(solution)/shard_map/pallas_call | solution.py:73
  1.2 0.6 collective-permute-start.2
  1.8 0.1 slice_bitcast_fusion
  1.9 0.7 %collective-permute-start = (bf16[544,512]{1,0:T(8,128)(2,1)S(1)}, bf16[544,512]{1,0:T(8,128)(2,1)S(1)}, u32[]{:S(2)}, u32[]{:S(2)}) collective-permute-start(bf16[544,512]{1,0:T(8,128)(2,1)S(1)} %pad_maximum_fusion), channel_id=1, source_target_pairs={{0,2},{2,0},{4,6},{6,4},{8,10},{10,8},{12,14},{14,12},{3,7},{7,11}... | collective-permute-start | bytes 1671176 | tf_op jit(solution)/shard_map/ppermute | solution.py:289
  2.6 0.1 slice.10
  2.7 0.7 %collective-permute-start.1 = (bf16[1024,512]{1,0:T(8,128)(2,1)S(1)}, bf16[1024,512]{1,0:T(8,128)(2,1)S(1)}, u32[]{:S(2)}, u32[]{:S(2)}) collective-permute-start(bf16[1024,512]{1,0:T(8,128)(2,1)S(1)} %bitcast.5), channel_id=1, source_target_pairs={{0,2},{2,0},{4,6},{6,4},{8,10},{10,8},{12,14},{14,12},{3,7},{7,11}... | collective-permute-start | bytes 3145736 | tf_op jit(solution)/shard_map/ppermute | solution.py:289
  3.4 0.7 %collective-permute-start.6 = (bf16[512,512]{1,0:T(8,128)(2,1)S(1)}, bf16[512,512]{1,0:T(8,128)(2,1)S(1)}, u32[]{:S(2)}, u32[]{:S(2)}) collective-permute-start(bf16[512,512]{1,0:T(8,128)(2,1)S(1)} %get-tuple-element.27), channel_id=1, source_target_pairs={{0,2},{2,0},{4,6},{6,4},{8,10},{10,8},{12,14},{14,12},{3,7},{7,11}... | collective-permute-start | bytes 1572872 | tf_op jit(solution)/shard_map/ppermute | solution.py:289
  4.1 0.1 collective-permute-done.2.send1_ref
  4.2 0.2 collective-permute-done.3.p1_ref
  4.4 11.4 %shard_map.74.refs_7_.refs_4_ = f32[2,2,512,512]{3,2,1,0:T(8,128)S(1)} custom-call(f32[512,8]{1,0:T(8,128)S(1)} %get-tuple-element.16.recv_ref, f32[8,512]{1,0:T(8,128)S(1)} %get-tuple-element.18.send0_ref, f32[8,512]{1,0:T(8,128)S(1)} %collective-permute-done.2.send1_ref, bf16[2,2,512,512]{3,2,1,0:T(8,128)(2,1)S(1)} %copy-done, ...), custom_call_target="tpu_custom_call" | custom-call | flops 103079215104 | bytes 1 | tf_op jit(solution)/shard_map/pallas_call | solution.py:163
  15.8 0.0 collective-permute-done.rest_2_.refs_4_
  15.8 0.0 collective-permute-done.1.refs_3_
  15.8 1.3 %collective-permute-start.5 = (bf16[1024,512]{1,0:T(8,128)(2,1)S(1)}, bf16[1024,512]{1,0:T(8,128)(2,1)S(1)}, u32[]{:S(2)}, u32[]{:S(2)}) collective-permute-start(bf16[1024,512]{1,0:T(8,128)(2,1)S(1)} %collective-permute-done.1.refs_3_), channel_id=1, source_target_pairs={{0,1},{4,5},{8,9},{12,13},{16,17},{20,21},{24,25},{28,29}} | collective-permute-start | bytes 3145736 | tf_op jit(solution)/shard_map/ppermute | solution.py:289
  17.1 10.8 %collective-permute-start.4 = (bf16[544,512]{1,0:T(8,128)(2,1)S(1)}, bf16[544,512]{1,0:T(8,128)(2,1)S(1)}, u32[]{:S(2)}, u32[]{:S(2)}) collective-permute-start(bf16[544,512]{1,0:T(8,128)(2,1)S(1)} %collective-permute-done.rest_2_.refs_4_), channel_id=1, source_target_pairs={{1,2},{3,1},{0,4},{6,3},{5,6},{7,5},{4,8},{10,7},{9,10},{11,9},{8,... | collective-permute-start | bytes 1671176 | tf_op jit(solution)/shard_map/ppermute | solution.py:289
  27.9 1.3 %collective-permute-start.11 = (bf16[544,512]{1,0:T(8,128)(2,1)S(1)}, bf16[544,512]{1,0:T(8,128)(2,1)S(1)}, u32[]{:S(2)}, u32[]{:S(2)}) collective-permute-start(bf16[544,512]{1,0:T(8,128)(2,1)S(1)} %collective-permute-done.rest_2_.refs_4_), channel_id=1, source_target_pairs={{0,1},{4,5},{8,9},{12,13},{16,17},{20,21},{24,25},{28,29}} | collective-permute-start | bytes 1671176 | tf_op jit(solution)/shard_map/ppermute | solution.py:289
  29.2 1.3 %collective-permute-start.7 = (bf16[512,512]{1,0:T(8,128)(2,1)S(1)}, bf16[512,512]{1,0:T(8,128)(2,1)S(1)}, u32[]{:S(2)}, u32[]{:S(2)}) collective-permute-start(bf16[512,512]{1,0:T(8,128)(2,1)S(1)} %collective-permute-done.6.refs_3_), channel_id=1, source_target_pairs={{0,1},{4,5},{8,9},{12,13},{16,17},{20,21},{24,25},{28,29}} | collective-permute-start | bytes 1572872 | tf_op jit(solution)/shard_map/ppermute | solution.py:289
  30.5 4.8 %collective-permute-start.10 = (bf16[1024,512]{1,0:T(8,128)(2,1)S(1)}, bf16[1024,512]{1,0:T(8,128)(2,1)S(1)}, u32[]{:S(2)}, u32[]{:S(2)}) collective-permute-start(bf16[1024,512]{1,0:T(8,128)(2,1)S(1)} %collective-permute-done.1.refs_3_), channel_id=1, source_target_pairs={{1,2},{3,1},{0,4},{6,3},{5,6},{7,5},{4,8},{10,7},{9,10},{11,9},{8,... | collective-permute-start | bytes 3145736 | tf_op jit(solution)/shard_map/ppermute | solution.py:289
  35.2 0.7 %collective-permute-start.9 = (bf16[512,512]{1,0:T(8,128)(2,1)S(1)}, bf16[512,512]{1,0:T(8,128)(2,1)S(1)}, u32[]{:S(2)}, u32[]{:S(2)}) collective-permute-start(bf16[512,512]{1,0:T(8,128)(2,1)S(1)} %collective-permute-done.6.refs_3_), channel_id=1, source_target_pairs={{1,2},{3,1},{0,4},{6,3},{5,6},{7,5},{4,8},{10,7},{9,10},{11,9},{8,... | collective-permute-start | bytes 1572872 | tf_op jit(solution)/shard_map/ppermute | solution.py:289
  35.9 0.8 %collective-permute-done.4.rest_1_.rest_0_.refs_2_.refs_6_ = bf16[544,512]{1,0:T(8,128)(2,1)S(1)} collective-permute-done((bf16[544,512]{1,0:T(8,128)(2,1)S(1)}, bf16[544,512]{1,0:T(8,128)(2,1)S(1)}, u32[]{:S(2)}, u32[]{:S(2)}) %collective-permute-start.4) | collective-permute-done | bytes 557088 | tf_op jit(solution)/shard_map/ppermute | solution.py:289
  36.7 4.7 %collective-permute-start.8 = (bf16[544,512]{1,0:T(8,128)(2,1)S(1)}, bf16[544,512]{1,0:T(8,128)(2,1)S(1)}, u32[]{:S(2)}, u32[]{:S(2)}) collective-permute-start(bf16[544,512]{1,0:T(8,128)(2,1)S(1)} %collective-permute-done.4.rest_1_.rest_0_.refs_2_.refs_6_), channel_id=1, source_target_pairs={{1,0},{2,3},{5,4},{6,7},{9,8},{10,11},{13,12},{14,15},{17,16},{18,... | collective-permute-start | bytes 1671176 | tf_op jit(solution)/shard_map/ppermute | solution.py:289
  41.4 3.4 %shard_map.76.refs_0_ = bf16[2,2,512,512]{3,2,1,0:T(8,128)(2,1)S(1)} custom-call(f32[512,8]{1,0:T(8,128)S(1)} %get-tuple-element.16.recv_ref, bf16[544,512]{1,0:T(8,128)(2,1)S(1)} %collective-permute-done.4.rest_1_.rest_0_.refs_2_.refs_6_, bf16[544,512]{1,0:T(8,128)(2,1)S(1)} %collective-permute-done.11.rest_1_.refs_3_, ...), custom_call_target="tpu_custom_call" | custom-call | flops 34359738368 | bytes 1 | tf_op jit(solution)/shard_map/pallas_call | solution.py:192
  44.9 3.4 %shard_map.75.refs_1_.refs_0_.kern_ref = bf16[2,2,512,512]{3,2,1,0:T(8,128)(2,1)S(1)} custom-call(f32[512,8]{1,0:T(8,128)S(1)} %get-tuple-element.16.recv_ref, bf16[544,512]{1,0:T(8,128)(2,1)S(1)} %collective-permute-done.8.rest_0_.refs_5_, bf16[544,512]{1,0:T(8,128)(2,1)S(1)} %collective-permute-done.4.rest_1_.rest_0_.refs_2_.refs_6_), custom_call_target="tpu_custom_call" | custom-call | flops 34359738368 | bytes 1 | tf_op jit(solution)/shard_map/pallas_call | solution.py:192
  48.3 1.3 %shard_map.77.refs_4_ = f32[2,512,512]{2,1,0:T(8,128)S(1)} custom-call(bf16[2,2,512,512]{3,2,1,0:T(8,128)(2,1)S(1)} %shard_map.76.refs_0_, bf16[2,2,512,512]{3,2,1,0:T(8,128)(2,1)S(1)} %shard_map.75.refs_1_.refs_0_.kern_ref, bf16[544,512]{1,0:T(8,128)(2,1)S(1)} %collective-permute-done.4.rest_1_.rest_0_.refs_2_.refs_6_, ...), custom_call_target="tpu_custom_call" | custom-call | flops 17179869184 | bytes 1 | tf_op jit(solution)/shard_map/pallas_call | solution.py:245
  49.6 4.8 %collective-permute-start.12 = (bf16[1024,512]{1,0:T(8,128)(2,1)S(1)}, bf16[1024,512]{1,0:T(8,128)(2,1)S(1)}, u32[]{:S(2)}, u32[]{:S(2)}) collective-permute-start(bf16[1024,512]{1,0:T(8,128)(2,1)S(1)} %collective-permute-done.10.refs_1_.refs_2_), channel_id=1, source_target_pairs={{1,0},{2,3},{5,4},{6,7},{9,8},{10,11},{13,12},{14,15},{17,16},{18,... | collective-permute-start | bytes 3145736 | tf_op jit(solution)/shard_map/ppermute | solution.py:289
  54.5 1.3 %shard_map.78.refs_3_ = f32[2,512,512]{2,1,0:T(8,128)S(1)} custom-call(bf16[2,2,512,512]{3,2,1,0:T(8,128)(2,1)S(1)} %shard_map.76.refs_0_, bf16[1024,512]{1,0:T(8,128)(2,1)S(1)} %collective-permute-done.10.refs_1_.refs_2_, bf16[1024,512]{1,0:T(8,128)(2,1)S(1)} %collective-permute-done.5.refs_2_, bf16[1024,512]{1,0:T(8,128)(2,1)S(1)} %collective-permute-done.1.refs_3_, ...), custom_call_target="tpu_custom_call" | custom-call | flops 17179869184 | bytes 1 | tf_op jit(solution)/shard_map/pallas_call | solution.py:245
  55.8 0.9 %collective-permute-done.12.refs_1_ = bf16[1024,512]{1,0:T(8,128)(2,1)S(1)} collective-permute-done((bf16[1024,512]{1,0:T(8,128)(2,1)S(1)}, bf16[1024,512]{1,0:T(8,128)(2,1)S(1)}, u32[]{:S(2)}, u32[]{:S(2)}) %collective-permute-start.12) | collective-permute-done | bytes 1048608 | tf_op jit(solution)/shard_map/ppermute | solution.py:289
  56.7 2.6 %shard_map.79.whole_ref = f32[2,2,512,512]{3,2,1,0:T(8,128)} custom-call(bf16[2,2,512,512]{3,2,1,0:T(8,128)(2,1)S(1)} %shard_map.75.refs_1_.refs_0_.kern_ref, bf16[1024,512]{1,0:T(8,128)(2,1)S(1)} %collective-permute-done.12.refs_1_, bf16[1024,512]{1,0:T(8,128)(2,1)S(1)} %collective-permute-done.10.refs_1_.refs_2_, f32[2,512,512]{2,1,0:T(8,128)S(1)} %shard_map.78.refs_3_), custom_call_target="tpu_custom_call" | custom-call | flops 17179869184 | bytes 1 | tf_op jit(solution)/shard_map/pallas_call | solution.py:245
  59.3 2.3 %collective-permute-start.13 = (bf16[512,512]{1,0:T(8,128)(2,1)S(1)}, bf16[512,512]{1,0:T(8,128)(2,1)S(1)}, u32[]{:S(2)}, u32[]{:S(2)}) collective-permute-start(bf16[512,512]{1,0:T(8,128)(2,1)S(1)} %collective-permute-done.9.refs_1_.y_ref), channel_id=1, source_target_pairs={{1,0},{2,3},{5,4},{6,7},{9,8},{10,11},{13,12},{14,15},{17,16},{18,... | collective-permute-start | bytes 1572872 | tf_op jit(solution)/shard_map/ppermute | solution.py:289
  61.6 0.7 %shard_map.80.acc_ref = f32[2,512,512]{2,1,0:T(8,128)S(1)} custom-call(bf16[2,2,512,512]{3,2,1,0:T(8,128)(2,1)S(1)} %shard_map.76.refs_0_, bf16[512,512]{1,0:T(8,128)(2,1)S(1)} %collective-permute-done.9.refs_1_.y_ref, bf16[512,512]{1,0:T(8,128)(2,1)S(1)} %collective-permute-done.7.refs_2_, bf16[512,512]{1,0:T(8,128)(2,1)S(1)} %collective-permute-done.6.refs_3_, ...), custom_call_target="tpu_custom_call" | custom-call | flops 17179869184 | bytes 1 | tf_op jit(solution)/shard_map/pallas_call | solution.py:245
  62.3 0.8 %collective-permute-done.13.x_ref = bf16[512,512]{1,0:T(8,128)(2,1)S(1)} collective-permute-done((bf16[512,512]{1,0:T(8,128)(2,1)S(1)}, bf16[512,512]{1,0:T(8,128)(2,1)S(1)}, u32[]{:S(2)}, u32[]{:S(2)}) %collective-permute-start.13) | collective-permute-done | bytes 524320 | tf_op jit(solution)/shard_map/ppermute | solution.py:289
  63.1 1.9 %shard_map.81 = f32[2,2,512,512]{3,2,1,0:T(8,128)} custom-call(bf16[2,2,512,512]{3,2,1,0:T(8,128)(2,1)S(1)} %shard_map.75.refs_1_.refs_0_.kern_ref, bf16[512,512]{1,0:T(8,128)(2,1)S(1)} %collective-permute-done.13.x_ref, bf16[512,512]{1,0:T(8,128)(2,1)S(1)} %collective-permute-done.9.refs_1_.y_ref, ...), custom_call_target="tpu_custom_call", output_to_operand_aliasing={{}: (4, {})} | custom-call | flops 17179869184 | bytes 1 | tf_op jit(solution)/shard_map/pallas_call | solution.py:275
  (10 shorter events, 0.1 us)
Async XLA Ops:
  0.0 1.8 %copy-start = (bf16[2,2,512,512]{3,2,1,0:T(8,128)(2,1)S(1)}, bf16[2,2,512,512]{3,2,1,0:T(8,128)(2,1)}, u32[]{:S(2)}) copy-start(bf16[2,2,512,512]{3,2,1,0:T(8,128)(2,1)} %p0_ref.1) | copy-start | bytes 6291460
  0.0 4.4 %collective-permute-start.3 = (bf16[2,2,512,512]{3,2,1,0:T(8,128)(2,1)}, bf16[2,2,512,512]{3,2,1,0:T(8,128)(2,1)S(1)}, u32[]{:S(2)}, u32[]{:S(2)}) collective-permute-start(bf16[2,2,512,512]{3,2,1,0:T(8,128)(2,1)} %p0_ref.1), channel_id=1, source_target_pairs={{0,1},{1,0},{2,3},{3,2},{4,5},{5,4},{6,7},{7,6},{8,9},{9,8},{10,11... | collective-permute-start | bytes 6291464 | tf_op jit(solution)/shard_map/ppermute | solution.py:289
  1.2 3.0 %collective-permute-start.2 = (f32[8,512]{1,0:T(8,128)S(1)}, f32[8,512]{1,0:T(8,128)S(1)}, u32[]{:S(2)}, u32[]{:S(2)}) collective-permute-start(f32[8,512]{1,0:T(8,128)S(1)} %get-tuple-element.18.send0_ref), channel_id=1, source_target_pairs={{0,1},{1,0},{2,3},{3,2},{4,5},{5,4},{6,7},{7,6},{8,9},{9,8},{10,11... | collective-permute-start | bytes 49160 | tf_op jit(solution)/shard_map/ppermute | solution.py:289
  1.9 13.9 %collective-permute-start = (bf16[544,512]{1,0:T(8,128)(2,1)S(1)}, bf16[544,512]{1,0:T(8,128)(2,1)S(1)}, u32[]{:S(2)}, u32[]{:S(2)}) collective-permute-start(bf16[544,512]{1,0:T(8,128)(2,1)S(1)} %pad_maximum_fusion), channel_id=1, source_target_pairs={{0,2},{2,0},{4,6},{6,4},{8,10},{10,8},{12,14},{14,12},{3,7},{7,11}... | collective-permute-start | bytes 1671176 | tf_op jit(solution)/shard_map/ppermute | solution.py:289
  2.7 13.1 %collective-permute-start.1 = (bf16[1024,512]{1,0:T(8,128)(2,1)S(1)}, bf16[1024,512]{1,0:T(8,128)(2,1)S(1)}, u32[]{:S(2)}, u32[]{:S(2)}) collective-permute-start(bf16[1024,512]{1,0:T(8,128)(2,1)S(1)} %bitcast.5), channel_id=1, source_target_pairs={{0,2},{2,0},{4,6},{6,4},{8,10},{10,8},{12,14},{14,12},{3,7},{7,11}... | collective-permute-start | bytes 3145736 | tf_op jit(solution)/shard_map/ppermute | solution.py:289
  3.4 25.7 %collective-permute-start.6 = (bf16[512,512]{1,0:T(8,128)(2,1)S(1)}, bf16[512,512]{1,0:T(8,128)(2,1)S(1)}, u32[]{:S(2)}, u32[]{:S(2)}) collective-permute-start(bf16[512,512]{1,0:T(8,128)(2,1)S(1)} %get-tuple-element.27), channel_id=1, source_target_pairs={{0,2},{2,0},{4,6},{6,4},{8,10},{10,8},{12,14},{14,12},{3,7},{7,11}... | collective-permute-start | bytes 1572872 | tf_op jit(solution)/shard_map/ppermute | solution.py:289
  15.8 20.8 %collective-permute-start.5 = (bf16[1024,512]{1,0:T(8,128)(2,1)S(1)}, bf16[1024,512]{1,0:T(8,128)(2,1)S(1)}, u32[]{:S(2)}, u32[]{:S(2)}) collective-permute-start(bf16[1024,512]{1,0:T(8,128)(2,1)S(1)} %collective-permute-done.1.refs_3_), channel_id=1, source_target_pairs={{0,1},{4,5},{8,9},{12,13},{16,17},{20,21},{24,25},{28,29}} | collective-permute-start | bytes 3145736 | tf_op jit(solution)/shard_map/ppermute | solution.py:289
  17.1 19.5 %collective-permute-start.4 = (bf16[544,512]{1,0:T(8,128)(2,1)S(1)}, bf16[544,512]{1,0:T(8,128)(2,1)S(1)}, u32[]{:S(2)}, u32[]{:S(2)}) collective-permute-start(bf16[544,512]{1,0:T(8,128)(2,1)S(1)} %collective-permute-done.rest_2_.refs_4_), channel_id=1, source_target_pairs={{1,2},{3,1},{0,4},{6,3},{5,6},{7,5},{4,8},{10,7},{9,10},{11,9},{8,... | collective-permute-start | bytes 1671176 | tf_op jit(solution)/shard_map/ppermute | solution.py:289
  27.9 13.5 %collective-permute-start.11 = (bf16[544,512]{1,0:T(8,128)(2,1)S(1)}, bf16[544,512]{1,0:T(8,128)(2,1)S(1)}, u32[]{:S(2)}, u32[]{:S(2)}) collective-permute-start(bf16[544,512]{1,0:T(8,128)(2,1)S(1)} %collective-permute-done.rest_2_.refs_4_), channel_id=1, source_target_pairs={{0,1},{4,5},{8,9},{12,13},{16,17},{20,21},{24,25},{28,29}} | collective-permute-start | bytes 1671176 | tf_op jit(solution)/shard_map/ppermute | solution.py:289
  29.2 6.1 %collective-permute-start.7 = (bf16[512,512]{1,0:T(8,128)(2,1)S(1)}, bf16[512,512]{1,0:T(8,128)(2,1)S(1)}, u32[]{:S(2)}, u32[]{:S(2)}) collective-permute-start(bf16[512,512]{1,0:T(8,128)(2,1)S(1)} %collective-permute-done.6.refs_3_), channel_id=1, source_target_pairs={{0,1},{4,5},{8,9},{12,13},{16,17},{20,21},{24,25},{28,29}} | collective-permute-start | bytes 1572872 | tf_op jit(solution)/shard_map/ppermute | solution.py:289
  30.5 19.1 %collective-permute-start.10 = (bf16[1024,512]{1,0:T(8,128)(2,1)S(1)}, bf16[1024,512]{1,0:T(8,128)(2,1)S(1)}, u32[]{:S(2)}, u32[]{:S(2)}) collective-permute-start(bf16[1024,512]{1,0:T(8,128)(2,1)S(1)} %collective-permute-done.1.refs_3_), channel_id=1, source_target_pairs={{1,2},{3,1},{0,4},{6,3},{5,6},{7,5},{4,8},{10,7},{9,10},{11,9},{8,... | collective-permute-start | bytes 3145736 | tf_op jit(solution)/shard_map/ppermute | solution.py:289
  35.2 24.0 %collective-permute-start.9 = (bf16[512,512]{1,0:T(8,128)(2,1)S(1)}, bf16[512,512]{1,0:T(8,128)(2,1)S(1)}, u32[]{:S(2)}, u32[]{:S(2)}) collective-permute-start(bf16[512,512]{1,0:T(8,128)(2,1)S(1)} %collective-permute-done.6.refs_3_), channel_id=1, source_target_pairs={{1,2},{3,1},{0,4},{6,3},{5,6},{7,5},{4,8},{10,7},{9,10},{11,9},{8,... | collective-permute-start | bytes 1572872 | tf_op jit(solution)/shard_map/ppermute | solution.py:289
  36.7 8.2 %collective-permute-start.8 = (bf16[544,512]{1,0:T(8,128)(2,1)S(1)}, bf16[544,512]{1,0:T(8,128)(2,1)S(1)}, u32[]{:S(2)}, u32[]{:S(2)}) collective-permute-start(bf16[544,512]{1,0:T(8,128)(2,1)S(1)} %collective-permute-done.4.rest_1_.rest_0_.refs_2_.refs_6_), channel_id=1, source_target_pairs={{1,0},{2,3},{5,4},{6,7},{9,8},{10,11},{13,12},{14,15},{17,16},{18,... | collective-permute-start | bytes 1671176 | tf_op jit(solution)/shard_map/ppermute | solution.py:289
  49.6 7.1 %collective-permute-start.12 = (bf16[1024,512]{1,0:T(8,128)(2,1)S(1)}, bf16[1024,512]{1,0:T(8,128)(2,1)S(1)}, u32[]{:S(2)}, u32[]{:S(2)}) collective-permute-start(bf16[1024,512]{1,0:T(8,128)(2,1)S(1)} %collective-permute-done.10.refs_1_.refs_2_), channel_id=1, source_target_pairs={{1,0},{2,3},{5,4},{6,7},{9,8},{10,11},{13,12},{14,15},{17,16},{18,... | collective-permute-start | bytes 3145736 | tf_op jit(solution)/shard_map/ppermute | solution.py:289
  59.3 3.8 %collective-permute-start.13 = (bf16[512,512]{1,0:T(8,128)(2,1)S(1)}, bf16[512,512]{1,0:T(8,128)(2,1)S(1)}, u32[]{:S(2)}, u32[]{:S(2)}) collective-permute-start(bf16[512,512]{1,0:T(8,128)(2,1)S(1)} %collective-permute-done.9.refs_1_.y_ref), channel_id=1, source_target_pairs={{1,0},{2,3},{5,4},{6,7},{9,8},{10,11},{13,12},{14,15},{17,16},{18,... | collective-permute-start | bytes 1572872 | tf_op jit(solution)/shard_map/ppermute | solution.py:289
